TPU v7x, 32 devices: a whole 2x2x4 slice. The times are simulated.
32 devices in a mesh: stream: 2 (over y), seq: 8 (over z, core), tensor: 2 (over x).
Axes of the slice: x: 2, y: 2, z: 4, core: 2. Of those that a mesh axis runs over, the one named last changes fastest.
Arguments:
- hidden: bfloat16 [2, 1, 4096, 4096], P('stream', None, 'seq', 'tensor'), may hold values from -32 to 32
- norm_gain: float32 [4096], replicated, may hold values from 0.1 to 1.9
- query_weight: bfloat16 [4096, 4096], P('seq', 'tensor'), may hold values from -1 to 1
- key_weight: bfloat16 [4096, 1024], P('seq', 'tensor'), may hold values from -24 to 24
- value_projection_weight: bfloat16 [4096, 1024], P('seq', 'tensor'), may hold values from -0.09375 to 0.09375
- out_weight: bfloat16 [4096, 4096], P('tensor', 'seq'), may hold values from -0.125 to 0.125
Outputs:
- cross_out: bfloat16 [2, 1, 4096, 4096], P('stream', None, 'seq', 'tensor')
All inputs are finite; a program needn't handle non-finite values.
Results may differ from a plain program's by a relative error of at most 0.014.
The roundings to bfloat16 on the way count: a program that leaves them out, or rounds other values in their place, can miss the bound.
Values may be sent and summed in bfloat16 or wider, within the bound.
A program may use at most 256 MiB of HBM per device.

v0:
```python
import jax
import jax.numpy as jnp
from jax import lax
from jax.sharding import PartitionSpec as P

HEAD_DIM = 128


def swapped(block, axis, stride):
    count = lax.axis_size(axis)
    route = []
    for low in range(count):
        high = low | 1 << stride
        if high != low and high < count:
            route += [(low, high), (high, low)]
    return lax.ppermute(block, axis, route)


def online_update(running, query_heads, key_block, value_block, query_frame):
    maximum, totals, accumulated = running
    windows, key_count, key_width = key_block.shape
    heads_kv = query_heads.shape[1]
    head_size = query_heads.shape[3]
    key_heads = key_block.reshape(windows, key_count, heads_kv, head_size)
    value_heads = value_block.reshape(windows, key_count, heads_kv, head_size)
    scores = jnp.einsum(
        "bkrd,bnkd->bkrn", query_heads, key_heads, preferred_element_type=jnp.float32
    ) * head_size ** (-0.5)
    key_frame = jnp.arange(key_count, dtype=jnp.int32)
    allowed = key_frame[None, :] <= query_frame[:, None]
    scores = jnp.where(allowed, scores, -1e30)
    fresh = jnp.maximum(maximum, jnp.max(scores, axis=-1))
    expo = jnp.where(allowed, jnp.exp(scores - fresh[..., None]), 0.0)
    totals = jnp.sum(expo, axis=-1)
    product = jnp.einsum(
        "bkrn,bnkd->bkrd",
        expo.astype(jnp.bfloat16),
        value_heads,
        preferred_element_type=jnp.float32,
    )
    accumulated = product
    return (fresh, totals, accumulated)


def body(hidden, norm_gain, query_weight, key_weight, value_projection_weight, out_weight):
    windows = hidden.shape[1]
    frame_count = hidden.shape[2]
    gathered = lax.all_gather(hidden, "tensor", axis=3, tiled=True)
    model_width = gathered.shape[3]
    flat_rows = gathered.reshape(windows * frame_count, model_width).astype(jnp.float32)
    inverse_rms = lax.rsqrt(jnp.mean(flat_rows * flat_rows, axis=1, keepdims=True) + 1e-05)
    normed = (flat_rows * inverse_rms * norm_gain).astype(jnp.bfloat16)
    full_query, full_key, full_value, full_out = (
        lax.all_gather(query_weight, "seq", axis=0, tiled=True),
        lax.all_gather(key_weight, "seq", axis=0, tiled=True),
        lax.all_gather(value_projection_weight, "seq", axis=0, tiled=True),
        lax.all_gather(out_weight, "seq", axis=1, tiled=True),
    )
    query_sum = jnp.dot(normed, full_query, preferred_element_type=jnp.float32)
    key_sum = jnp.dot(normed, full_key, preferred_element_type=jnp.float32)
    value_sum = jnp.dot(normed, full_value, preferred_element_type=jnp.float32)
    query_rows = query_sum.astype(jnp.bfloat16)
    self_key_rows = key_sum.astype(jnp.bfloat16).reshape(windows, frame_count, key_weight.shape[1])
    self_value_rows = value_sum.astype(jnp.bfloat16).reshape(
        windows, frame_count, value_projection_weight.shape[1]
    )
    partner_keys, partner_values = swapped((self_key_rows, self_value_rows), "stream", 0)
    heads_kv = key_weight.shape[1] // HEAD_DIM
    group_repeat = query_weight.shape[1] // (heads_kv * HEAD_DIM)
    query_heads = (
        query_rows.reshape(windows, frame_count, heads_kv, group_repeat, HEAD_DIM)
        .transpose(0, 2, 3, 1, 4)
        .reshape(windows, heads_kv, group_repeat * frame_count, HEAD_DIM)
    )
    query_start = lax.axis_index("seq") * frame_count
    query_frame = query_start + jnp.tile(jnp.arange(frame_count, dtype=jnp.int32), group_repeat)
    initial = (
        jnp.full((windows, heads_kv, group_repeat * frame_count), -1e30, jnp.float32),
        jnp.zeros((windows, heads_kv, group_repeat * frame_count), jnp.float32),
        jnp.zeros((windows, heads_kv, group_repeat * frame_count, HEAD_DIM), jnp.float32),
    )
    query_end = query_start + frame_count
    pieces = (
        lax.all_gather(partner_keys, "seq", axis=1, tiled=True),
        lax.all_gather(partner_values, "seq", axis=1, tiled=True),
    )

    def taken(current):
        return online_update(current, query_heads, pieces[0], pieces[1], query_frame)

    def skipped(current):
        return current

    maximum, totals, accumulated = lax.cond(jnp.int32(0) < query_end, taken, skipped, initial)
    attended_output = (accumulated / totals[..., None]).astype(jnp.bfloat16)
    attended_output = (
        attended_output.reshape(windows, heads_kv, group_repeat, frame_count, HEAD_DIM)
        .transpose(0, 3, 1, 2, 4)
        .reshape(windows * frame_count, heads_kv * group_repeat * HEAD_DIM)
    )
    partial_out = jnp.dot(attended_output, full_out, preferred_element_type=jnp.float32)
    summed = lax.psum_scatter(
        partial_out.astype(jnp.bfloat16), "tensor", scatter_dimension=1, tiled=True
    ).astype(jnp.float32)
    return summed.astype(jnp.bfloat16).reshape(1, windows, frame_count, summed.shape[1])


def solution(mesh):
    in_specs = (
        P("stream", None, "seq", "tensor"),
        P(),
        P("seq", "tensor"),
        P("seq", "tensor"),
        P("seq", "tensor"),
        P("tensor", "seq"),
    )
    out_specs = P("stream", None, "seq", "tensor")
    return jax.shard_map(body, mesh=mesh, in_specs=in_specs, out_specs=out_specs, check_vma=False)
```

profile of v0, /device:TPU:29, one launch (start us, length us, event | category | flops | bytes accessed | tf_op | source)
XLA Modules:
  0.0 663.3 jit_solution(13722145855826253714)
XLA Ops:
  6.5 0.0 copy-start.3
  6.5 0.0 all-gather.8.cloned.1.call-start
  6.5 0.7 all-gather.8.cloned.1.call-update
  7.3 0.0 all-gather.12.cloned.1.call-start
  7.3 0.7 all-gather.12.cloned.1.call-update
  8.0 0.0 all-gather.16.cloned.1.call-start
  8.1 0.7 all-gather.16.cloned.1.call-update
  8.7 0.0 all-gather.10.cloned.1.call-start
  8.8 0.5 all-gather.10.cloned.1.call-update
  9.3 0.0 all-gather.14.cloned.1.call-start
  9.4 57.2 %all-gather.8.cloned.1.call-done = bf16[1,1,512,4096]{3,2,1,0:T(8,128)(2,1)} async-done(((bf16[1,1,512,2048]{3,2,1,0:T(8,128)(2,1)}), bf16[1,1,512,4096]{3,2,1,0:T(8,128)(2,1)}) %all-gather.8.cloned.1.call-update) | async-done | bytes 4194320 | tf_op jit(solution)/shard_map/all_gather | solution.py:48
  66.6 3.1 fusion.17
  69.7 43.9 %all-gather.12.cloned.1.call-done = bf16[4096,512]{1,0:T(8,128)(2,1)} async-done(((bf16[512,512]{1,0:T(8,128)(2,1)}), bf16[4096,512]{1,0:T(8,128)(2,1)}) %all-gather.12.cloned.1.call-update) | async-done | bytes 4194320 | tf_op jit(solution)/shard_map/all_gather | solution.py:55
  113.6 0.0 copy-done.3
  113.6 5.8 fusion.20
  119.5 0.3 collective-permute-start
  119.8 13.1 %collective-permute-done = bf16[1,512,512]{2,1,0:T(8,128)(2,1)S(1)} collective-permute-done((bf16[1,512,512]{2,1,0:T(8,128)(2,1)S(1)}, bf16[1,512,512]{2,1,0:T(8,128)(2,1)S(1)}, u32[]{:S(2)}, u32[]{:S(2)}) %collective-permute-start) | collective-permute-done | bytes 524320 | tf_op jit(solution)/shard_map/ppermute | solution.py:16
  132.9 0.8 copy-done.1
  133.7 0.0 all-gather.14.cloned.1.call-update
  133.7 0.0 all-gather.18.cloned.1.call-start
  133.8 27.3 %all-gather.16.cloned.1.call-done = bf16[4096,512]{1,0:T(8,128)(2,1)} async-done(((bf16[512,512]{1,0:T(8,128)(2,1)}), bf16[4096,512]{1,0:T(8,128)(2,1)}) %all-gather.16.cloned.1.call-update) | async-done | bytes 4194320 | tf_op jit(solution)/shard_map/all_gather | solution.py:56
  161.1 5.8 fusion.21
  167.0 0.3 collective-permute-start.1
  167.3 13.1 %collective-permute-done.1 = bf16[1,512,512]{2,1,0:T(8,128)(2,1)S(1)} collective-permute-done((bf16[1,512,512]{2,1,0:T(8,128)(2,1)S(1)}, bf16[1,512,512]{2,1,0:T(8,128)(2,1)S(1)}, u32[]{:S(2)}, u32[]{:S(2)}) %collective-permute-start.1) | collective-permute-done | bytes 524320 | tf_op jit(solution)/shard_map/ppermute | solution.py:16
  180.4 0.8 copy-done.2
  181.2 0.0 all-gather.18.cloned.1.call-update
  181.2 0.0 all-gather.20.cloned.1.call-start
  181.3 0.7 all-gather.20.cloned.1.call-update
  182.0 0.2 reduce-scatter.2.cloned.1.call-start
  182.2 129.7 %all-gather.10.cloned.1.call-done = bf16[4096,2048]{1,0:T(8,128)(2,1)} async-done(((bf16[512,2048]{1,0:T(8,128)(2,1)}), bf16[4096,2048]{1,0:T(8,128)(2,1)}) %all-gather.10.cloned.1.call-update) | async-done | bytes 16777232 | tf_op jit(solution)/shard_map/all_gather | solution.py:54
  311.9 14.6 %convolution_convert_fusion.1 = bf16[512,2048]{1,0:T(8,128)(2,1)} fusion(bf16[4096,2048]{1,0:T(8,128)(2,1)} %all-gather.10.cloned.1.call-done, bf16[1,1,512,4096]{3,2,1,0:T(8,128)(2,1)} %all-gather.8.cloned.1.call-done, f32[4096]{0:T(1024)S(1)} %copy-done.3, f32[512]{0:T(512)S(1)} %add_rsqrt_fusion), kind=kOutput, calls=%fused_computation.24 | convolution fusion | flops 8599371776 | bytes 23087104 | tf_op jit(solution)/shard_map/dot_general | solution.py:59
  326.5 3.2 reshape.72
  329.8 1.9 copy.27
  331.6 27.6 %all-gather.14.cloned.1.call-done = bf16[1,4096,512]{2,1,0:T(8,128)(2,1)} async-done(((bf16[1,512,512]{2,1,0:T(8,128)(2,1)}), bf16[1,4096,512]{2,1,0:T(8,128)(2,1)}) %all-gather.14.cloned.1.call-update) | async-done | bytes 4194320 | tf_op jit(solution)/shard_map/all_gather | solution.py:84
  359.2 47.4 %all-gather.18.cloned.1.call-done = bf16[1,4096,512]{2,1,0:T(8,128)(2,1)} async-done(((bf16[1,512,512]{2,1,0:T(8,128)(2,1)}), bf16[1,4096,512]{2,1,0:T(8,128)(2,1)}) %all-gather.18.cloned.1.call-update) | async-done | bytes 4194320 | tf_op jit(solution)/shard_map/all_gather | solution.py:85
  406.6 174.1 %conditional.1 = (f32[1,4,2048]{2,1,0:T(4,128)}, f32[1,4,2048,128]{3,2,1,0:T(8,128)}) conditional(s32[]{:T(128)} %convert_element_type.33, () %tuple.13, (s32[]{:T(128)}, s32[4,512]{1,0:T(4,128)S(1)}, bf16[1,4,4,512,128]{4,3,2,1,0:T(8,128)(2,1)}, bf16[1,4096,512]{2,1,0:T(8,128)(2,1)}, bf16[1,4096,512]{2,1,0:T(8,128)(2,1)}) %tuple.34), branch_computations={%region_1.0_spmd, %region_2.5_spmd} | conditional | flops 17624459264 | bytes 476291136 | solution.py:94
  406.7 10.4 %iota_compare_fusion = pred[2048,4096]{1,0:T(8,128)(4,1)} fusion(s32[2048]{0:T(1024)S(1)} %bitcast.37), kind=kLoop, calls=%fused_computation.7 | loop fusion | flops 8388608 | bytes 8396800 | tf_op jit(solution)/shard_map/cond/branch_1_fun/le | solution.py:30
  417.0 7.3 %reshape.64 = bf16[4096,4,128]{2,1,0:T(4,128)(2,1)} reshape(bf16[1,4096,512]{2,1,0:T(8,128)(2,1)} %get-tuple-element.22) | data formatting | bytes 8388608 | tf_op jit(solution)/shard_map/reshape.1
  424.3 0.0 copy-done
  424.3 50.8 %fusion = (f32[4,2048]{1,0:T(4,128)S(1)}, f32[4,2048,4096]{2,1,0:T(8,128)}) fusion(pred[2048,4096]{1,0:T(8,128)(4,1)} %iota_compare_fusion, bf16[4,2048,128]{2,1,0:T(8,128)(2,1)S(1)} %bitcast.35, bf16[4096,4,128]{2,1,0:T(4,128)(2,1)} %reshape.64), kind=kOutput, calls=%fused_computation.2 | convolution fusion | flops 8690589696 | bytes 148930560 | tf_op jit(solution)/shard_map/cond/branch_1_fun/bkrd,bnkd->bkrn/dot_general | solution.py:26
  475.1 7.0 %reshape.65 = bf16[4096,4,128]{2,1,0:T(4,128)(2,1)} reshape(bf16[1,4096,512]{2,1,0:T(8,128)(2,1)} %get-tuple-element.23) | data formatting | bytes 8388608 | tf_op jit(solution)/shard_map/reshape.5
  482.1 54.1 %fusion.9 = f32[1,4,2048,128]{3,2,1,0:T(8,128)} fusion(bf16[4096,4,128]{2,1,0:T(4,128)(2,1)} %reshape.65, f32[4,2048,4096]{2,1,0:T(8,128)} %get-tuple-element.29, f32[4,2048]{1,0:T(4,128)S(1)} %broadcast_maximum_fusion, pred[2048,4096]{1,0:T(8,128)(4,1)} %iota_compare_fusion), kind=kOutput, calls=%fused_computation.11 | convolution fusion | flops 8757706752 | bytes 151027712 | tf_op jit(solution)/shard_map/cond/branch_1_fun/bkrn,bnkd->bkrd/dot_general | solution.py:35
  536.2 44.5 %fusion.2 = f32[4,2048]{1,0:T(4,128)} fusion(f32[4,2048,4096]{2,1,0:T(8,128)} %get-tuple-element.29, f32[4,2048]{1,0:T(4,128)S(1)} %broadcast_maximum_fusion, pred[2048,4096]{1,0:T(8,128)(4,1)} %iota_compare_fusion), kind=kLoop, calls=%fused_computation.4 | loop fusion | flops 167763968 | bytes 142671872 | tf_op jit(solution)/shard_map/cond/branch_1_fun/reduce_sum | solution.py:34
  580.8 2.9 divide_convert_fusion
  583.7 2.3 copy.16
  586.0 14.5 %convolution_convert_fusion = bf16[512,4096]{1,0:T(8,128)(2,1)} fusion(bf16[512,2048]{0,1:T(8,128)(2,1)} %bitcast.36, bf16[2048,4096]{1,0:T(8,128)(2,1)} %all-gather.20.cloned.1.call-done), kind=kOutput, calls=%fused_computation.22 | convolution fusion | flops 8592031744 | bytes 23068672 | tf_op jit(solution)/shard_map/dot_general | solution.py:101
  600.5 0.0 reduce-scatter.2.cloned.1.call-update
  600.5 56.0 %reduce-scatter.2.cloned.1.call-done = bf16[512,2048]{1,0:T(8,128)(2,1)} async-done(((bf16[512,4096]{1,0:T(8,128)(2,1)}), bf16[512,2048]{1,0:T(8,128)(2,1)}) %reduce-scatter.2.cloned.1.call-update) | async-done | bytes 2097168 | tf_op jit(solution)/shard_map/reduce_scatter | solution.py:102
  (9 shorter events, 0.0 us)
Async XLA Ops:
  6.5 107.1 %copy-start.3 = (f32[4096]{0:T(1024)S(1)}, f32[4096]{0:T(1024)}, u32[]{:S(2)}) copy-start(f32[4096]{0:T(1024)} %param.9) | copy-start | bytes 49156
  6.5 60.1 %all-gather.8.cloned.1.call-start = ((), (), s32[]{:S(2)}) async-start(), calls=%async_computation.1 | async-start | bytes 6291456 | tf_op jit(solution)/shard_map/all_gather | solution.py:48
  7.3 106.4 %all-gather.12.cloned.1.call-start = ((), (), s32[]{:S(2)}) async-start(), calls=%async_computation.3 | async-start | bytes 4718592 | tf_op jit(solution)/shard_map/all_gather | solution.py:55
  8.0 153.1 %all-gather.16.cloned.1.call-start = ((), (), s32[]{:S(2)}) async-start(), calls=%async_computation.5 | async-start | bytes 4718592 | tf_op jit(solution)/shard_map/all_gather | solution.py:56
  8.7 303.1 %all-gather.10.cloned.1.call-start = ((), (), s32[]{:S(2)}) async-start(), calls=%async_computation.2 | async-start | bytes 18874368 | tf_op jit(solution)/shard_map/all_gather | solution.py:54
  9.3 349.9 %all-gather.14.cloned.1.call-start = ((), (), s32[]{:S(2)}) async-start(), calls=%async_computation.4 | async-start | bytes 4718592 | tf_op jit(solution)/shard_map/all_gather | solution.py:84
  119.5 13.4 %collective-permute-start = (bf16[1,512,512]{2,1,0:T(8,128)(2,1)S(1)}, bf16[1,512,512]{2,1,0:T(8,128)(2,1)S(1)}, u32[]{:S(2)}, u32[]{:S(2)}) collective-permute-start(bf16[1,512,512]{2,1,0:T(8,128)(2,1)S(1)} %fusion.20), channel_id=1, source_target_pairs={{0,16},{16,0},{1,17},{17,1},{2,18},{18,2},{3,19},{19,3},{4,20},{20... | collective-permute-start | bytes 1572872 | tf_op jit(solution)/shard_map/ppermute | solution.py:16
  132.9 0.8 copy-start.1
  133.7 272.9 %all-gather.18.cloned.1.call-start = ((), (), s32[]{:S(2)}) async-start(), calls=%async_computation.6 | async-start | bytes 4718592 | tf_op jit(solution)/shard_map/all_gather | solution.py:85
  167.0 13.4 %collective-permute-start.1 = (bf16[1,512,512]{2,1,0:T(8,128)(2,1)S(1)}, bf16[1,512,512]{2,1,0:T(8,128)(2,1)S(1)}, u32[]{:S(2)}, u32[]{:S(2)}) collective-permute-start(bf16[1,512,512]{2,1,0:T(8,128)(2,1)S(1)} %fusion.21), channel_id=1, source_target_pairs={{0,16},{16,0},{1,17},{17,1},{2,18},{18,2},{3,19},{19,3},{4,20},{20... | collective-permute-start | bytes 1572872 | tf_op jit(solution)/shard_map/ppermute | solution.py:16
  180.4 0.8 copy-start.2
  181.2 404.8 %all-gather.20.cloned.1.call-start = ((), (), s32[]{:S(2)}) async-start(), calls=%async_computation.7 | async-start | bytes 18874368 | tf_op jit(solution)/shard_map/all_gather | solution.py:57
  182.0 474.5 %reduce-scatter.2.cloned.1.call-start = ((), (), s32[]{:S(2)}) async-start(), calls=%async_computation.8 | async-start | bytes 6291456 | tf_op jit(solution)/shard_map/reduce_scatter | solution.py:102
  406.7 17.7 %copy-start = (bf16[1,4,4,512,128]{4,3,2,1,0:T(8,128)(2,1)S(1)}, bf16[1,4,4,512,128]{4,3,2,1,0:T(8,128)(2,1)}, u32[]{:S(2)}) copy-start(bf16[1,4,4,512,128]{4,3,2,1,0:T(8,128)(2,1)} %get-tuple-element.21) | copy-start | bytes 6291460 | tf_op jit(solution)/shard_map/cond
Sparse Core Ops, SparseCore 0:
  8.9 57.6 all-gather.7
  68.2 45.3 all-gather.11
  115.2 45.8 all-gather.15
  162.6 149.2 all-gather.9
  313.3 45.8 all-gather.13
  360.7 45.9 all-gather.17
  408.2 149.1 all-gather.19
  600.6 55.7 reduce-scatter.1
where the time goes:
time: 666 us; the launch traced here: 663 us
  waiting for transfers between devices  419 us (63%)
  matrix products  146 us (22%)
  other arithmetic  60.9 us (9%)
  local copies, waits for them, and re-layouts  23.3 us (3%)
  between operations  13.5 us (2%)
    all_gather x1, waiting for transfers between devices, body(): lax.all_gather(query_weight, 'seq', axis=0, tiled=True)  130 us
    all_gather x1, waiting for transfers between devices, body(): gathered = lax.all_gather(hidden, 'tensor', axis=3, tiled=True)  57.2 us
    reduce_scatter x1, waiting for transfers between devices, body(): lax.psum_scatter(partial_out.astype(jnp.bfloat16), 'tensor', scatter_dime...  56 us
    dot_general x1, matrix products, online_update(): jnp.einsum('bkrn,bnkd->bkrd', expo.astype(jnp.bfloat16), value_heads, pre...  54.1 us
    dot_general x1, matrix products, online_update(): jnp.einsum('bkrd,bnkd->bkrn', query_heads, key_heads, preferred_element_t...  50.8 us
    all_gather x1, waiting for transfers between devices, body(): lax.all_gather(partner_values, 'seq', axis=1, tiled=True)  47.4 us
    reduce_sum x1, other arithmetic, online_update(): totals = jnp.sum(expo, axis=-1)  44.5 us
    all_gather x1, waiting for transfers between devices, body(): lax.all_gather(key_weight, 'seq', axis=0, tiled=True)  43.9 us
  transfers between devices with their start and end apart: 10, of which 9 were waited for; matrix products, arithmetic and copies ran while one was open for 32% of the time, Pallas kernels for 0%

commit v1 on v0

v1 whole, which is shorter than its diff:
```python
import functools

import jax
import jax.numpy as jnp
from jax import lax
from jax.experimental import pallas as pl
from jax.experimental.pallas import tpu as pltpu
from jax.sharding import PartitionSpec as P

HEAD_DIM = 128
ROW_CHUNKS = 2
KEY_BLOCK = 512
LOG2E = 1.4426950408889634


def swap_pairs(block, axis):
    count = lax.axis_size(axis)
    return lax.ppermute(block, axis, [(i, i ^ 1) for i in range(count)])


def attend_kernel(repeat, start_ref, q_ref, k_ref, v_ref, o_ref, m_ref, l_ref, acc_ref):
    step = pl.program_id(1)
    rows = q_ref.shape[0]
    keys = k_ref.shape[0]
    start = start_ref[0]
    last = (start + rows - 1) // keys
    scale = LOG2E * HEAD_DIM ** (-0.5)

    @pl.when(step == 0)
    def _():
        m_ref[...] = jnp.full_like(m_ref, -1e30)
        l_ref[...] = jnp.zeros_like(l_ref)
        acc_ref[...] = jnp.zeros_like(acc_ref)

    def update(masked):
        k = k_ref[...]
        v = v_ref[...]
        if masked:
            frame = start + lax.broadcasted_iota(jnp.int32, (rows, keys), 0)
            key = step * keys + lax.broadcasted_iota(jnp.int32, (rows, keys), 1)
            allowed = key <= frame
        for r in range(repeat):
            q = q_ref[:, r * HEAD_DIM:(r + 1) * HEAD_DIM]
            s = lax.dot_general(q, k, (((1,), (1,)), ((), ())), preferred_element_type=jnp.float32)
            if masked:
                s = jnp.where(allowed, s, -1e30)
            top = jnp.max(s, axis=1, keepdims=True) * scale
            before = m_ref[r]
            fresh = jnp.maximum(before, top)
            m_ref[r] = fresh
            alpha = jnp.exp2(before - fresh)
            p = jnp.exp2(s * scale - fresh[:, :1])
            part = p[:, :HEAD_DIM]
            for j in range(1, keys // HEAD_DIM):
                part = part + p[:, j * HEAD_DIM:(j + 1) * HEAD_DIM]
            l_ref[r] = alpha * l_ref[r] + part
            acc_ref[r] = alpha * acc_ref[r] + jnp.dot(
                p.astype(jnp.bfloat16), v, preferred_element_type=jnp.float32
            )

    @pl.when(step < last)
    def _():
        update(False)

    @pl.when(step == last)
    def _():
        update(True)
        for r in range(repeat):
            totals = jnp.sum(l_ref[r], axis=1, keepdims=True)
            o_ref[:, r * HEAD_DIM:(r + 1) * HEAD_DIM] = (acc_ref[r] / totals).astype(o_ref.dtype)


def attend(start, queries, keys_values, repeat):
    rows, width = queries.shape
    count = keys_values.shape[0]
    groups = width // (repeat * HEAD_DIM)
    block = min(KEY_BLOCK, count)

    def at(step, start_ref):
        return jnp.minimum(step, (start_ref[0] + rows - 1) // block)

    return pl.pallas_call(
        functools.partial(attend_kernel, repeat),
        out_shape=jax.ShapeDtypeStruct((rows, width), jnp.bfloat16),
        grid_spec=pltpu.PrefetchScalarGridSpec(
            num_scalar_prefetch=1,
            grid=(groups, count // block),
            in_specs=[
                pl.BlockSpec((rows, repeat * HEAD_DIM), lambda g, i, s: (0, g)),
                pl.BlockSpec((block, HEAD_DIM), lambda g, i, s: (at(i, s), g)),
                pl.BlockSpec((block, HEAD_DIM), lambda g, i, s: (at(i, s), groups + g)),
            ],
            out_specs=pl.BlockSpec((rows, repeat * HEAD_DIM), lambda g, i, s: (0, g)),
            scratch_shapes=[
                pltpu.VMEM((repeat, rows, HEAD_DIM), jnp.float32),
                pltpu.VMEM((repeat, rows, HEAD_DIM), jnp.float32),
                pltpu.VMEM((repeat, rows, HEAD_DIM), jnp.float32),
            ],
        ),
        compiler_params=pltpu.CompilerParams(
            dimension_semantics=("arbitrary", "arbitrary"), vmem_limit_bytes=32 * 1024 * 1024
        ),
        cost_estimate=pl.CostEstimate(
            flops=8 * rows * count * width,
            bytes_accessed=2 * (2 * rows * width + keys_values.size),
            transcendentals=rows * count * width // HEAD_DIM,
        ),
    )(start.reshape(1), queries, keys_values, keys_values)


def y_share(mine, core):
    depth = mine.shape[0] // 2
    part = lax.dynamic_slice_in_dim(mine, core * depth, depth, 0)
    near = lax.ppermute(part, "stream", [(0, 1), (1, 0)])
    far = swap_pairs(near, "seq")
    return near, far


def body(hidden, norm_gain, query_weight, key_weight, value_projection_weight, out_weight):
    windows, frame_count = hidden.shape[1], hidden.shape[2]
    n_tensor = lax.axis_size("tensor")
    n_seq = lax.axis_size("seq")
    stream = lax.axis_index("stream")
    tensor = lax.axis_index("tensor")
    seq = lax.axis_index("seq")
    core = seq % 2
    rows = windows * frame_count
    depth = query_weight.shape[0] // 2
    out_half = out_weight.shape[1] // 2

    kv_weight = jnp.concatenate([key_weight, value_projection_weight], axis=1)
    kv_mine = lax.all_gather(
        lax.dynamic_slice_in_dim(kv_weight, stream * depth, depth, 0), "seq", axis=0, tiled=True
    )
    query_half, kv_mine = lax.optimization_barrier(
        (lax.dynamic_slice_in_dim(query_weight, stream * depth, depth, 0), kv_mine)
    )
    query_mine = lax.all_gather(query_half, "seq", axis=0, tiled=True)
    out_piece, query_mine = lax.optimization_barrier(
        (lax.dynamic_slice_in_dim(out_weight, stream * out_half, out_half, 1), query_mine)
    )
    out_mine = lax.all_gather(out_piece, "seq", axis=1, tiled=True)

    local = hidden.reshape(rows, hidden.shape[3])
    if n_tensor == 2:
        other = lax.ppermute(local, "tensor", [(0, 1), (1, 0)])
        gathered = jnp.where(
            tensor == 0,
            jnp.concatenate([local, other], axis=1),
            jnp.concatenate([other, local], axis=1),
        )
    else:
        gathered = lax.all_gather(local, "tensor", axis=1, tiled=True)
    flat = gathered.astype(jnp.float32)
    inverse_rms = lax.rsqrt(jnp.mean(flat * flat, axis=1, keepdims=True) + 1e-05)
    normed = (flat * inverse_rms * norm_gain).astype(jnp.bfloat16)
    split = normed.reshape(rows, n_seq, 2, depth)

    def features(half):
        return lax.dynamic_index_in_dim(split, half, 2, keepdims=False).reshape(rows, n_seq * depth)

    normed_mine = features(stream)
    normed_other = features(1 - stream)
    span = n_seq * depth // 2
    normed_near = lax.dynamic_slice_in_dim(normed_other, core * span, span, 1)
    normed_far = lax.dynamic_slice_in_dim(normed_other, (1 - core) * span, span, 1)

    def project(mine, near, far):
        total = jnp.dot(normed_mine, mine, preferred_element_type=jnp.float32)
        total += jnp.dot(normed_near, near, preferred_element_type=jnp.float32)
        total += jnp.dot(normed_far, far, preferred_element_type=jnp.float32)
        return total.astype(jnp.bfloat16)

    keys_values = project(kv_mine, *y_share(kv_mine, core))
    partner = lax.ppermute(keys_values, "stream", [(0, 1), (1, 0)])
    partner, out_mine = lax.optimization_barrier((partner, out_mine))
    pieces = lax.all_gather(
        partner.reshape(windows, frame_count, partner.shape[1]), "seq", axis=1, tiled=True
    )
    queries = project(query_mine, *y_share(query_mine, core)).reshape(windows, frame_count, -1)
    out_near, out_far = y_share(out_mine, core)
    width = out_weight.shape[0] // 2

    repeat = query_weight.shape[1] // key_weight.shape[1]
    chunk = frame_count // ROW_CHUNKS

    def scattered(share):
        if n_tensor == 2:
            wide = share.shape[1] // 2
            away = lax.dynamic_slice_in_dim(share, (1 - tensor) * wide, wide, 1)
            kept = lax.dynamic_slice_in_dim(share, tensor * wide, wide, 1)
            came = lax.ppermute(away, "tensor", [(0, 1), (1, 0)])
            return (kept.astype(jnp.float32) + came.astype(jnp.float32)).astype(jnp.bfloat16)
        return lax.psum_scatter(share, "tensor", scatter_dimension=1, tiled=True)

    outs = []
    for window in range(windows):
        for index in range(ROW_CHUNKS):
            start = seq * frame_count + index * chunk
            attended = attend(
                start,
                lax.slice_in_dim(queries[window], index * chunk, (index + 1) * chunk, axis=0),
                pieces[window],
                repeat,
            )
            share_mine = jnp.dot(attended, out_mine, preferred_element_type=jnp.float32)
            attended_near = lax.dynamic_slice_in_dim(attended, core * width, width, 1)
            attended_far = lax.dynamic_slice_in_dim(attended, (1 - core) * width, width, 1)
            share_other = jnp.dot(attended_near, out_near, preferred_element_type=jnp.float32)
            share_other += jnp.dot(attended_far, out_far, preferred_element_type=jnp.float32)
            mine = scattered(share_mine.astype(jnp.bfloat16)).reshape(chunk, -1, out_half)
            other = scattered(share_other.astype(jnp.bfloat16)).reshape(chunk, -1, out_half)
            outs.append(
                jnp.where(
                    stream == 0, jnp.stack([mine, other], axis=2), jnp.stack([other, mine], axis=2)
                ).reshape(chunk, -1)
            )
    return jnp.concatenate(outs, axis=0).reshape(1, windows, frame_count, -1)


def solution(mesh):
    in_specs = (
        P("stream", None, "seq", "tensor"),
        P(),
        P("seq", "tensor"),
        P("seq", "tensor"),
        P("seq", "tensor"),
        P("tensor", "seq"),
    )
    out_specs = P("stream", None, "seq", "tensor")
    return jax.shard_map(body, mesh=mesh, in_specs=in_specs, out_specs=out_specs, check_vma=False)
```

time: 666 us -> 615 us (0.923)
  Pallas kernels: 0 us -> 129 us
  matrix products: 146 us -> 46.2 us
  waiting for transfers between devices: 419 us -> 359 us
  other arithmetic: 60.9 us -> 16.1 us
  local copies, waits for them, and re-layouts: 23.3 us -> 33.9 us
  starting transfers between devices: 1.14 us -> 10.4 us
    all_gather x7 -> x4, waiting for transfers between devices: 333 us -> 125 us  [the longest x1 79.8 us: body(): query_mine = lax.all_gather(query_half, 'seq', axis=0, tiled=True)]
    ppermute x2 -> x12, waiting for transfers between devices: 26.2 us -> 233 us  [the longest x3 208 us: y_share(): near = lax.ppermute(part, 'stream', [(0, 1), (1, 0)])]
    pallas_call x0 -> x2, Pallas kernels: none -> 129 us  [attend(): pl.pallas_call(functools.partial(attend_kernel, repeat), out_shape=jax.Sh...]
    dot_general x6 -> x12, matrix products: 146 us -> 46.2 us  [the longest x2 10.1 us: project(): total = jnp.dot(normed_mine, mine, preferred_element_type=jnp.float32)]
    reduce_scatter x1 -> x0, waiting for transfers between devices: 56 us -> none  [body(): lax.psum_scatter(partial_out.astype(jnp.bfloat16), 'tensor', scatter_dime...]
    reduce_sum x2 -> x1, other arithmetic: 47.6 us -> 3.1 us  [body(): jnp.mean(flat * flat, axis=1, keepdims=True) + 1e-05]
    dynamic_slice x0 -> x10, local copies, waits for them, and re-layouts: none -> 13.6 us  [the longest x3 8.07 us: y_share(): part = lax.dynamic_slice_in_dim(mine, core * depth, depth, 0)]
    another operation x3 -> x4, local copies, waits for them, and re-layouts: 14.3 us -> 1.5 us  [body(): jnp.stack([mine, other], axis=2)]
  transfers between devices with their start and end apart: 10 -> 16, of which waited for: 9 -> 7; matrix products, arithmetic and copies ran while one was open for 32% -> 13% of each run, Pallas kernels for 0% -> 21%
where the time goes in v1:
time: 615 us; the launch traced here: 608 us
  waiting for transfers between devices  359 us (58%)
  Pallas kernels  129 us (21%)
  matrix products  46.2 us (8%)
  local copies, waits for them, and re-layouts  33.9 us (6%)
  other arithmetic  16.1 us (3%)
  between operations  14 us (2%)
  starting transfers between devices  10.4 us (2%)
    ppermute x3, waiting for transfers between devices, y_share(): near = lax.ppermute(part, 'stream', [(0, 1), (1, 0)])  208 us
    pallas_call x2, Pallas kernels, attend(): pl.pallas_call(functools.partial(attend_kernel, repeat), out_shape=jax.Sh...  129 us
    all_gather x1, waiting for transfers between devices, body(): query_mine = lax.all_gather(query_half, 'seq', axis=0, tiled=True)  79.8 us
    all_gather x1, waiting for transfers between devices, body(): lax.all_gather(lax.dynamic_slice_in_dim(kv_weight, stream * depth, depth,...  45.6 us
    ppermute x1, waiting for transfers between devices, body(): partner = lax.ppermute(keys_values, 'stream', [(0, 1), (1, 0)])  24.8 us
  transfers between devices with their start and end apart: 16, of which 7 were waited for; matrix products, arithmetic and copies ran while one was open for 13% of the time, Pallas kernels for 21%

profile of v1, /device:TPU:29, one launch (start us, length us, event | category | flops | bytes accessed | tf_op | source)
XLA Modules:
  0.0 608.2 jit_solution(5621030520973569496)
XLA Ops:
  6.5 2.0 fusion.8
  8.6 1.1 constant_dynamic-slice_fusion.8
  9.7 45.6 %all-gather.6.cloned.1.call-done = bf16[2048,1024]{1,0:T(8,128)(2,1)} async-done(((bf16[256,1024]{1,0:T(8,128)(2,1)}), bf16[2048,1024]{1,0:T(8,128)(2,1)}) %all-gather.6.cloned.1.call-update) | async-done | bytes 4194320 | tf_op jit(solution)/shard_map/all_gather | solution.py:132
  55.4 2.3 constant_dynamic-slice_fusion.9
  57.6 79.8 %all-gather.8.cloned.1.call-done = bf16[2048,2048]{1,0:T(8,128)(2,1)} async-done(((bf16[256,2048]{1,0:T(8,128)(2,1)}), bf16[2048,2048]{1,0:T(8,128)(2,1)}) %all-gather.8.cloned.1.call-update) | async-done | bytes 8388624 | tf_op jit(solution)/shard_map/all_gather | solution.py:138
  137.5 2.9 copy.11
  140.4 3.1 constant_dynamic-slice_fusion.5
  143.5 1.4 collective-permute-start
  144.9 45.8 %collective-permute-done.3 = bf16[1024,1024]{1,0:T(8,128)(2,1)} collective-permute-done((bf16[1024,1024]{1,0:T(8,128)(2,1)}, bf16[1024,1024]{1,0:T(8,128)(2,1)}, u32[]{:S(2)}, u32[]{:S(2)}) %collective-permute-start.3) | collective-permute-done | bytes 2097184 | tf_op jit(solution)/shard_map/ppermute | solution.py:114
  190.7 1.1 collective-permute-start.4
  191.8 3.1 multiply_reduce_fusion
  194.9 3.2 multiply_convert_fusion
  198.4 2.7 copy-done.5
  201.1 2.3 fusion.25
  203.5 2.9 fusion.4
  206.4 1.4 add_convert_fusion.1
  207.9 24.8 %collective-permute-done.5 = bf16[512,1024]{1,0:T(8,128)(2,1)S(1)} collective-permute-done((bf16[512,1024]{1,0:T(8,128)(2,1)S(1)}, bf16[512,1024]{1,0:T(8,128)(2,1)S(1)}, u32[]{:S(2)}, u32[]{:S(2)}) %collective-permute-start.5) | collective-permute-done | bytes 1048608 | tf_op jit(solution)/shard_map/ppermute | solution.py:175
  232.6 1.0 copy-done.6
  233.6 2.7 constant_dynamic-slice_fusion.6
  236.4 1.9 copy-done.4
  238.3 2.3 constant_dynamic-slice_fusion.3
  240.6 87.2 %collective-permute-done.1 = bf16[1024,2048]{1,0:T(8,128)(2,1)} collective-permute-done((bf16[1024,2048]{1,0:T(8,128)(2,1)S(1)}, bf16[1024,2048]{1,0:T(8,128)(2,1)}, u32[]{:S(2)}, u32[]{:S(2)}) %collective-permute-start.1) | collective-permute-done | bytes 4194336 | tf_op jit(solution)/shard_map/ppermute | solution.py:114
  327.8 2.9 collective-permute-start.2
  330.7 7.8 %fusion.24 = f32[512,2048]{1,0:T(8,128)S(1)} fusion(bf16[512,2048]{0,1:T(8,128)(2,1)} %bitcast.35, bf16[2048,2048]{1,0:T(8,128)(2,1)} %all-gather.8.cloned.1.call-done), kind=kOutput, calls=%fused_computation.55 | convolution fusion | flops 4294967296 | bytes 14680064 | tf_op jit(solution)/shard_map/dot_general | solution.py:169
  338.5 4.7 fusion.6
  343.1 74.6 %collective-permute-done.7 = bf16[1024,2048]{1,0:T(8,128)(2,1)} collective-permute-done((bf16[1024,2048]{1,0:T(8,128)(2,1)}, bf16[1024,2048]{1,0:T(8,128)(2,1)}, u32[]{:S(2)}, u32[]{:S(2)}) %collective-permute-start.7) | collective-permute-done | bytes 4194336 | tf_op jit(solution)/shard_map/ppermute | solution.py:114
  417.7 1.6 collective-permute-start.8
  419.4 4.9 add_convert_fusion
  424.5 3.4 copy-done.2
  427.9 64.4 %shard_map.64 = bf16[256,2048]{1,0:T(8,128)(2,1)S(1)} custom-call(s32[1]{0:T(128)} %bitcast.start_ref, bf16[256,2048]{1,0:T(8,128)(2,1)S(1)} %get-tuple-element.19.q_ref, bf16[4096,1024]{1,0:T(8,128)(2,1)S(1)} %copy-done.2, bf16[4096,1024]{1,0:T(8,128)(2,1)S(1)} %copy-done.2), custom_call_target="tpu_custom_call" | custom-call | flops 17179869184 | bytes 10485760 | tf_op jit(solution)/shard_map/pallas_call | solution.py:82
  492.3 5.7 convolution_convert_fusion.1
  498.0 1.2 collective-permute-start.6
  499.2 3.6 fusion.13
  502.8 3.7 fusion
  507.0 64.6 %shard_map.65 = bf16[256,2048]{1,0:T(8,128)(2,1)S(1)} custom-call(s32[1]{0:T(128)} %bitcast.6.start_ref, bf16[256,2048]{1,0:T(8,128)(2,1)S(1)} %get-tuple-element.20.q_ref, bf16[4096,1024]{1,0:T(8,128)(2,1)S(1)} %bitcast.26, bf16[4096,1024]{1,0:T(8,128)(2,1)S(1)} %bitcast.26), custom_call_target="tpu_custom_call" | custom-call | flops 17179869184 | bytes 10485760 | tf_op jit(solution)/shard_map/pallas_call | solution.py:82
  571.6 2.4 convolution_convert_fusion
  574.1 0.9 constant_dynamic-slice_fusion.1
  575.0 1.1 collective-permute-start.10
  576.1 3.4 fusion.10
  579.5 3.5 fusion.1
  583.1 0.9 constant_dynamic-slice_fusion
  586.2 1.6 copy.13
  587.9 1.8 select_n.91
  589.7 1.4 add_convert_fusion.3
  592.3 1.4 add_convert_fusion.2
  594.8 1.6 copy.14
  596.5 1.6 select_n.93
  598.1 3.1 maximum_bitcast_fusion
  (64 shorter events, 6.0 us)
Async XLA Ops:
  6.5 2.1 copy-start
  6.5 48.7 %all-gather.6.cloned.1.call-start = ((), (), s32[]{:S(2)}) async-start(), calls=%async_computation | async-start | bytes 4718592 | tf_op jit(solution)/shard_map/all_gather | solution.py:132
  8.6 128.8 %all-gather.8.cloned.1.call-start = ((), (), s32[]{:S(2)}) async-start(), calls=%async_computation.1 | async-start | bytes 9437184 | tf_op jit(solution)/shard_map/all_gather | solution.py:138
  55.3 177.3 %all-gather.10.cloned.1.call-start = ((), (), s32[]{:S(2)}) async-start(), calls=%async_computation.2 | async-start | bytes 9437184 | tf_op jit(solution)/shard_map/all_gather | solution.py:142
  137.4 287.1 %all-gather.12.cloned.1.call-start = ((), (), s32[]{:S(2)}) async-start(), calls=%async_computation.3 | async-start | bytes 9437184 | tf_op jit(solution)/shard_map/all_gather | solution.py:177
  137.5 7.4 %copy-start.9 = (f32[4096]{0:T(1024)S(1)}, f32[4096]{0:T(1024)}, u32[]{:S(2)}) copy-start(f32[4096]{0:T(1024)} %param.7) | copy-start | bytes 49156
  143.5 47.3 %collective-permute-start.3 = (bf16[1024,1024]{1,0:T(8,128)(2,1)}, bf16[1024,1024]{1,0:T(8,128)(2,1)}, u32[]{:S(2)}, u32[]{:S(2)}) collective-permute-start(bf16[1024,1024]{1,0:T(8,128)(2,1)} %constant_dynamic-slice_fusion.5), channel_id=1, source_target_pairs={{0,16},{16,0},{1,17},{17,1},{2,18},{18,2},{3,19},{19,3},{4,20},{20... | collective-permute-start | bytes 6291464 | tf_op jit(solution)/shard_map/ppermute | solution.py:114
  143.5 48.3 %collective-permute-start = (bf16[512,2048]{0,1:T(8,128)(2,1)S(1)}, bf16[512,2048]{0,1:T(8,128)(2,1)}, u32[]{:S(2)}, u32[]{:S(2)}) collective-permute-start(bf16[512,2048]{0,1:T(8,128)(2,1)S(1)} %bitcast.27), channel_id=1, source_target_pairs={{0,1},{1,0},{2,3},{3,2},{4,5},{5,4},{6,7},{7,6},{8,9},{9,8},{10,11... | collective-permute-start | bytes 6291464 | tf_op jit(solution)/shard_map/ppermute | solution.py:146
  190.7 15.6 %collective-permute-start.4 = (bf16[1024,1024]{1,0:T(8,128)(2,1)}, bf16[1024,1024]{1,0:T(8,128)(2,1)S(1)}, u32[]{:S(2)}, u32[]{:S(2)}) collective-permute-start(bf16[1024,1024]{1,0:T(8,128)(2,1)} %collective-permute-done.3), channel_id=1, source_target_pairs={{0,2},{2,0},{4,6},{6,4},{8,10},{10,8},{12,14},{14,12},{1,3},{3,1},... | collective-permute-start | bytes 6291464 | tf_op jit(solution)/shard_map/ppermute | solution.py:18
  198.1 3.0 copy-start.5
  198.4 5.0 copy-start.3
  207.7 24.9 %collective-permute-start.5 = (bf16[512,1024]{1,0:T(8,128)(2,1)S(1)}, bf16[512,1024]{1,0:T(8,128)(2,1)S(1)}, u32[]{:S(2)}, u32[]{:S(2)}) collective-permute-start(bf16[512,1024]{1,0:T(8,128)(2,1)S(1)} %add_convert_fusion.1), channel_id=1, source_target_pairs={{0,16},{16,0},{1,17},{17,1},{2,18},{18,2},{3,19},{19,3},{4,20},{20... | collective-permute-start | bytes 3145736 | tf_op jit(solution)/shard_map/ppermute | solution.py:175
  232.6 1.0 copy-start.6
  233.6 4.6 copy-start.4
  236.3 91.5 %collective-permute-start.1 = (bf16[1024,2048]{1,0:T(8,128)(2,1)S(1)}, bf16[1024,2048]{1,0:T(8,128)(2,1)}, u32[]{:S(2)}, u32[]{:S(2)}) collective-permute-start(bf16[1024,2048]{1,0:T(8,128)(2,1)S(1)} %constant_dynamic-slice_fusion.6), channel_id=1, source_target_pairs={{0,16},{16,0},{1,17},{17,1},{2,18},{18,2},{3,19},{19,3},{4,20},{20... | collective-permute-start | bytes 12582920 | tf_op jit(solution)/shard_map/ppermute | solution.py:114
  240.6 177.1 %collective-permute-start.7 = (bf16[1024,2048]{1,0:T(8,128)(2,1)}, bf16[1024,2048]{1,0:T(8,128)(2,1)}, u32[]{:S(2)}, u32[]{:S(2)}) collective-permute-start(bf16[1024,2048]{1,0:T(8,128)(2,1)} %constant_dynamic-slice_fusion.3), channel_id=1, source_target_pairs={{0,16},{16,0},{1,17},{17,1},{2,18},{18,2},{3,19},{19,3},{4,20},{20... | collective-permute-start | bytes 12582920 | tf_op jit(solution)/shard_map/ppermute | solution.py:114
  327.8 91.5 %collective-permute-start.2 = (bf16[1024,2048]{1,0:T(8,128)(2,1)}, bf16[1024,2048]{1,0:T(8,128)(2,1)}, u32[]{:S(2)}, u32[]{:S(2)}) collective-permute-start(bf16[1024,2048]{1,0:T(8,128)(2,1)} %collective-permute-done.1), channel_id=1, source_target_pairs={{0,2},{2,0},{4,6},{6,4},{8,10},{10,8},{12,14},{14,12},{1,3},{3,1},... | collective-permute-start | bytes 12582920 | tf_op jit(solution)/shard_map/ppermute | solution.py:18
  417.7 85.1 %collective-permute-start.8 = (bf16[1024,2048]{1,0:T(8,128)(2,1)}, bf16[1024,2048]{1,0:T(8,128)(2,1)}, u32[]{:S(2)}, u32[]{:S(2)}) collective-permute-start(bf16[1024,2048]{1,0:T(8,128)(2,1)} %collective-permute-done.7), channel_id=1, source_target_pairs={{0,2},{2,0},{4,6},{6,4},{8,10},{10,8},{12,14},{14,12},{1,3},{3,1},... | collective-permute-start | bytes 12582920 | tf_op jit(solution)/shard_map/ppermute | solution.py:18
  424.5 3.4 copy-start.2
  498.0 86.3 %collective-permute-start.6 = (bf16[256,1024]{1,0:T(8,128)(2,1)S(1)}, bf16[256,1024]{1,0:T(8,128)(2,1)S(1)}, u32[]{:S(2)}, u32[]{:S(2)}) collective-permute-start(bf16[256,1024]{1,0:T(8,128)(2,1)S(1)} %constant_dynamic-slice_fusion.4), channel_id=1, source_target_pairs={{0,1},{1,0},{2,3},{3,2},{4,5},{5,4},{6,7},{7,6},{8,9},{9,8},{10,11... | collective-permute-start | bytes 1572872 | tf_op jit(solution)/shard_map/ppermute | solution.py:192
  499.2 7.7 %slice-start = ((s8[8388608]{0:T(1024)(128)(4,1)}), s8[4194304]{0:T(1024)(128)(4,1)S(1)}, s32[]{:S(2)}) async-start(s8[8388608]{0:T(1024)(128)(4,1)} %bitcast.25), calls=%async_computation.4 | async-start | bytes 8388608
  502.8 4.2 slice-start.1
  502.8 68.8 %slice-start.2 = ((s8[8388608]{0:T(1024)(128)(4,1)}), s8[4194304]{0:T(1024)(128)(4,1)S(1)}, s32[]{:S(2)}) async-start(s8[8388608]{0:T(1024)(128)(4,1)} %bitcast.36), calls=%async_computation.6 | async-start | bytes 8388608
  506.5 77.9 %collective-permute-start.9 = (bf16[256,1024]{1,0:T(8,128)(2,1)S(1)}, bf16[256,1024]{1,0:T(8,128)(2,1)S(1)}, u32[]{:S(2)}, u32[]{:S(2)}) collective-permute-start(bf16[256,1024]{1,0:T(8,128)(2,1)S(1)} %constant_dynamic-slice_fusion.2), channel_id=1, source_target_pairs={{0,1},{1,0},{2,3},{3,2},{4,5},{5,4},{6,7},{7,6},{8,9},{9,8},{10,11... | collective-permute-start | bytes 1572872 | tf_op jit(solution)/shard_map/ppermute | solution.py:192
  507.0 64.6 %slice-start.3 = ((s8[8388608]{0:T(1024)(128)(4,1)}), s8[4194304]{0:T(1024)(128)(4,1)S(1)}, s32[]{:S(2)}) async-start(s8[8388608]{0:T(1024)(128)(4,1)} %bitcast.36), calls=%async_computation.7 | async-start | bytes 8388608
  574.0 9.0 %copy-start.7 = (bf16[256,2048]{1,0:T(8,128)(2,1)}, bf16[256,2048]{1,0:T(8,128)(2,1)S(1)}, u32[]{:S(2)}) copy-start(bf16[256,2048]{1,0:T(8,128)(2,1)S(1)} %convolution_convert_fusion) | copy-start | bytes 3145732
  575.0 14.8 %collective-permute-start.10 = (bf16[256,1024]{1,0:T(8,128)(2,1)}, bf16[256,1024]{1,0:T(8,128)(2,1)}, u32[]{:S(2)}, u32[]{:S(2)}) collective-permute-start(bf16[256,1024]{1,0:T(8,128)(2,1)} %constant_dynamic-slice_fusion.1), channel_id=1, source_target_pairs={{0,1},{1,0},{2,3},{3,2},{4,5},{5,4},{6,7},{7,6},{8,9},{9,8},{10,11... | collective-permute-start | bytes 1572872 | tf_op jit(solution)/shard_map/ppermute | solution.py:192
  583.0 1.5 copy-start.8
  583.9 8.3 %collective-permute-start.11 = (bf16[256,1024]{1,0:T(8,128)(2,1)}, bf16[256,1024]{1,0:T(8,128)(2,1)}, u32[]{:S(2)}, u32[]{:S(2)}) collective-permute-start(bf16[256,1024]{1,0:T(8,128)(2,1)} %constant_dynamic-slice_fusion), channel_id=1, source_target_pairs={{0,1},{1,0},{2,3},{3,2},{4,5},{5,4},{6,7},{7,6},{8,9},{9,8},{10,11... | collective-permute-start | bytes 1572872 | tf_op jit(solution)/shard_map/ppermute | solution.py:192
  594.1 7.2 %copy-start.1 = (bf16[512,2048]{1,0:T(8,128)(2,1)S(1)}, bf16[512,2048]{1,0:T(8,128)(2,1)}, u32[]{:S(2)}) copy-start(bf16[512,2048]{1,0:T(8,128)(2,1)} %param.8) | copy-start | bytes 6291460
Sparse Core Ops, SparseCore 0:
  9.0 46.2 all-gather.5
  56.9 80.4 all-gather.7
  139.0 80.6 all-gather.9
  233.8 81.1 all-gather.11

commit v2 on v1

--- a/solution.py
+++ b/solution.py
@@ -9,7 +9,7 @@
 
 HEAD_DIM = 128
 ROW_CHUNKS = 2
-KEY_BLOCK = 512
+KEY_BLOCK = 1024
 LOG2E = 1.4426950408889634
 
 
@@ -36,26 +36,30 @@
         k = k_ref[...]
         v = v_ref[...]
         if masked:
-            frame = start + lax.broadcasted_iota(jnp.int32, (rows, keys), 0)
-            key = step * keys + lax.broadcasted_iota(jnp.int32, (rows, keys), 1)
+            frame = start + lax.broadcasted_iota(jnp.int32, (keys, rows), 1)
+            key = step * keys + lax.broadcasted_iota(jnp.int32, (keys, rows), 0)
             allowed = key <= frame
+
+        def scored(r):
+            q = q_ref[:, r * HEAD_DIM:(r + 1) * HEAD_DIM]
+            return lax.dot_general(k, q, (((1,), (1,)), ((), ())), preferred_element_type=jnp.float32)
+
+        following = scored(0)
         for r in range(repeat):
-            q = q_ref[:, r * HEAD_DIM:(r + 1) * HEAD_DIM]
-            s = lax.dot_general(q, k, (((1,), (1,)), ((), ())), preferred_element_type=jnp.float32)
+            s = following
+            if r + 1 < repeat:
+                following = scored(r + 1)
             if masked:
                 s = jnp.where(allowed, s, -1e30)
-            top = jnp.max(s, axis=1, keepdims=True) * scale
+            top = jnp.max(s, axis=0, keepdims=True) * scale
             before = m_ref[r]
             fresh = jnp.maximum(before, top)
             m_ref[r] = fresh
             alpha = jnp.exp2(before - fresh)
-            p = jnp.exp2(s * scale - fresh[:, :1])
-            part = p[:, :HEAD_DIM]
-            for j in range(1, keys // HEAD_DIM):
-                part = part + p[:, j * HEAD_DIM:(j + 1) * HEAD_DIM]
-            l_ref[r] = alpha * l_ref[r] + part
-            acc_ref[r] = alpha * acc_ref[r] + jnp.dot(
-                p.astype(jnp.bfloat16), v, preferred_element_type=jnp.float32
+            p = jnp.exp2(s * scale - fresh)
+            l_ref[r] = alpha * l_ref[r] + jnp.sum(p, axis=0, keepdims=True)
+            acc_ref[r] = alpha * acc_ref[r] + lax.dot_general(
+                v, p.astype(jnp.bfloat16), (((0,), (0,)), ((), ())), preferred_element_type=jnp.float32
             )
 
     @pl.when(step < last)
@@ -66,8 +70,8 @@
     def _():
         update(True)
         for r in range(repeat):
-            totals = jnp.sum(l_ref[r], axis=1, keepdims=True)
-            o_ref[:, r * HEAD_DIM:(r + 1) * HEAD_DIM] = (acc_ref[r] / totals).astype(o_ref.dtype)
+            attended = (acc_ref[r] / l_ref[r]).T
+            o_ref[:, r * HEAD_DIM:(r + 1) * HEAD_DIM] = attended.astype(o_ref.dtype)
 
 
 def attend(start, queries, keys_values, repeat):
@@ -92,9 +96,9 @@
             ],
             out_specs=pl.BlockSpec((rows, repeat * HEAD_DIM), lambda g, i, s: (0, g)),
             scratch_shapes=[
-                pltpu.VMEM((repeat, rows, HEAD_DIM), jnp.float32),
-                pltpu.VMEM((repeat, rows, HEAD_DIM), jnp.float32),
-                pltpu.VMEM((repeat, rows, HEAD_DIM), jnp.float32),
+                pltpu.VMEM((repeat, 1, rows), jnp.float32),
+                pltpu.VMEM((repeat, 1, rows), jnp.float32),
+                pltpu.VMEM((repeat, HEAD_DIM, rows), jnp.float32),
             ],
         ),
         compiler_params=pltpu.CompilerParams(
@@ -132,14 +136,12 @@
     kv_mine = lax.all_gather(
         lax.dynamic_slice_in_dim(kv_weight, stream * depth, depth, 0), "seq", axis=0, tiled=True
     )
-    query_half, kv_mine = lax.optimization_barrier(
-        (lax.dynamic_slice_in_dim(query_weight, stream * depth, depth, 0), kv_mine)
-    )
-    query_mine = lax.all_gather(query_half, "seq", axis=0, tiled=True)
-    out_piece, query_mine = lax.optimization_barrier(
-        (lax.dynamic_slice_in_dim(out_weight, stream * out_half, out_half, 1), query_mine)
-    )
-    out_mine = lax.all_gather(out_piece, "seq", axis=1, tiled=True)
+    query_mine = lax.all_gather(
+        lax.dynamic_slice_in_dim(query_weight, stream * depth, depth, 0), "seq", axis=0, tiled=True
+    )
+    out_mine = lax.all_gather(
+        lax.dynamic_slice_in_dim(out_weight, stream * out_half, out_half, 1), "seq", axis=1, tiled=True
+    )
 
     local = hidden.reshape(rows, hidden.shape[3])
     if n_tensor == 2:
@@ -173,10 +175,19 @@
 
     keys_values = project(kv_mine, *y_share(kv_mine, core))
     partner = lax.ppermute(keys_values, "stream", [(0, 1), (1, 0)])
-    partner, out_mine = lax.optimization_barrier((partner, out_mine))
-    pieces = lax.all_gather(
-        partner.reshape(windows, frame_count, partner.shape[1]), "seq", axis=1, tiled=True
-    )
+    kv_width = key_weight.shape[1]
+    parts = 2 if kv_width % (2 * HEAD_DIM) == 0 else 1
+    step = kv_width // parts
+    pieces = []
+    for part in range(parts):
+        columns = jnp.concatenate(
+            [partner[:, part * step:(part + 1) * step],
+             partner[:, kv_width + part * step:kv_width + (part + 1) * step]],
+            axis=1,
+        )
+        pieces.append(
+            lax.all_gather(columns.reshape(windows, frame_count, 2 * step), "seq", axis=1, tiled=True)
+        )
     queries = project(query_mine, *y_share(query_mine, core)).reshape(windows, frame_count, -1)
     out_near, out_far = y_share(out_mine, core)
     width = out_weight.shape[0] // 2
@@ -194,15 +205,26 @@
         return lax.psum_scatter(share, "tensor", scatter_dimension=1, tiled=True)
 
     outs = []
+    q_step = step * repeat
     for window in range(windows):
+        early = [
+            attend(
+                seq * frame_count,
+                queries[window][:, part * q_step:(part + 1) * q_step],
+                pieces[part][window],
+                repeat,
+            )
+            for part in range(parts - 1)
+        ]
         for index in range(ROW_CHUNKS):
-            start = seq * frame_count + index * chunk
-            attended = attend(
-                start,
-                lax.slice_in_dim(queries[window], index * chunk, (index + 1) * chunk, axis=0),
-                pieces[window],
+            low, high = index * chunk, (index + 1) * chunk
+            final = attend(
+                seq * frame_count + low,
+                queries[window][low:high, (parts - 1) * q_step:],
+                pieces[-1][window],
                 repeat,
             )
+            attended = jnp.concatenate([done[low:high] for done in early] + [final], axis=1)
             share_mine = jnp.dot(attended, out_mine, preferred_element_type=jnp.float32)
             attended_near = lax.dynamic_slice_in_dim(attended, core * width, width, 1)
             attended_far = lax.dynamic_slice_in_dim(attended, (1 - core) * width, width, 1)

time: 615 us -> 483 us (0.79)
  waiting for transfers between devices: 359 us -> 282 us
  Pallas kernels: 129 us -> 65.5 us
    pallas_call x2 -> x3, Pallas kernels: 129 us -> 65.5 us  [attend(): pl.pallas_call(functools.partial(attend_kernel, repeat), out_shape=jax.Sh...]
    ppermute x3, waiting for transfers between devices: 208 us -> 145 us  [y_share(): near = lax.ppermute(part, 'stream', [(0, 1), (1, 0)])]
    all_gather x3 -> x4, waiting for transfers between devices: 79.8 us -> 65.9 us  [the longest x1 65.8 us: body(): lax.all_gather(lax.dynamic_slice_in_dim(out_weight, stream * out_half, ou...]
    ppermute x4, waiting for transfers between devices: 0.77 us -> 7.12 us  [scattered(): came = lax.ppermute(away, 'tensor', [(0, 1), (1, 0)])]
  transfers between devices with their start and end apart: 16 -> 17, of which waited for: 7 -> 7; matrix products, arithmetic and copies ran while one was open for 13% -> 18% of each run, Pallas kernels for 21% -> 14%
where the time goes in v2:
time: 483 us; the launch traced here: 477 us
  waiting for transfers between devices  282 us (58%)
  Pallas kernels  65.5 us (14%)
  matrix products  46.1 us (10%)
  local copies, waits for them, and re-layouts  38 us (8%)
  other arithmetic  19.3 us (4%)
  between operations  13.8 us (3%)
  starting transfers between devices  11.6 us (2%)
    ppermute x3, waiting for transfers between devices, y_share(): near = lax.ppermute(part, 'stream', [(0, 1), (1, 0)])  145 us
    all_gather x1, waiting for transfers between devices, body(): lax.all_gather(lax.dynamic_slice_in_dim(out_weight, stream * out_half, ou...  65.8 us
    pallas_call x3, Pallas kernels, attend(): pl.pallas_call(functools.partial(attend_kernel, repeat), out_shape=jax.Sh...  65.5 us
    all_gather x1, waiting for transfers between devices, body(): lax.all_gather(lax.dynamic_slice_in_dim(kv_weight, stream * depth, depth,...  40.2 us
    ppermute x1, waiting for transfers between devices, body(): partner = lax.ppermute(keys_values, 'stream', [(0, 1), (1, 0)])  24.4 us
    dynamic_slice x3, local copies, waits for them, and re-layouts, y_share(): part = lax.dynamic_slice_in_dim(mine, core * depth, depth, 0)  13.1 us
    dot_general x2, matrix products, project(): total = jnp.dot(normed_mine, mine, preferred_element_type=jnp.float32)  9.96 us
    unnamed x21, local copies, waits for them, and re-layouts  9.93 us
  transfers between devices with their start and end apart: 17, of which 7 were waited for; matrix products, arithmetic and copies ran while one was open for 18% of the time, Pallas kernels for 14%

profile of v2, /device:TPU:29, one launch (start us, length us, event | category | flops | bytes accessed | tf_op | source)
XLA Modules:
  0.0 476.5 jit_solution(3644982112514395131)
XLA Ops:
  6.5 2.0 fusion.8
  8.6 1.1 constant_dynamic-slice_fusion.9
  9.8 2.3 constant_dynamic-slice_fusion.5
  12.2 2.9 copy.11
  15.1 40.2 %all-gather.10.cloned.1.call-done = bf16[2048,1024]{1,0:T(8,128)(2,1)} async-done(((bf16[256,1024]{1,0:T(8,128)(2,1)}), bf16[2048,1024]{1,0:T(8,128)(2,1)}) %all-gather.10.cloned.1.call-update) | async-done | bytes 4194320 | tf_op jit(solution)/shard_map/all_gather | solution.py:136
  55.3 3.1 constant_dynamic-slice_fusion.6
  58.6 1.2 collective-permute-start
  59.8 45.8 %collective-permute-done.3 = bf16[1024,1024]{1,0:T(8,128)(2,1)} collective-permute-done((bf16[1024,1024]{1,0:T(8,128)(2,1)}, bf16[1024,1024]{1,0:T(8,128)(2,1)}, u32[]{:S(2)}, u32[]{:S(2)}) %collective-permute-start.3) | collective-permute-done | bytes 2097184 | tf_op jit(solution)/shard_map/ppermute | solution.py:118
  106.7 3.1 multiply_reduce_fusion
  109.8 3.2 multiply_convert_fusion
  113.3 2.7 copy-done.5
  116.0 2.3 fusion.37
  118.4 2.9 fusion.4
  121.2 1.4 add_convert_fusion.1
  123.0 24.4 %collective-permute-done.5 = bf16[512,1024]{1,0:T(8,128)(2,1)S(1)} collective-permute-done((bf16[512,1024]{1,0:T(8,128)(2,1)S(1)}, bf16[512,1024]{1,0:T(8,128)(2,1)S(1)}, u32[]{:S(2)}, u32[]{:S(2)}) %collective-permute-start.5) | collective-permute-done | bytes 1048608 | tf_op jit(solution)/shard_map/ppermute | solution.py:177
  148.7 5.2 %constant_dynamic-slice_fusion.7 = bf16[1024,2048]{1,0:T(8,128)(2,1)} fusion(bf16[2048,2048]{1,0:T(8,128)(2,1)} %all-gather.8.cloned.1.call-done, s32[]{:T(128)S(6)} %select_n.86), kind=kLoop, calls=%fused_computation.60 | loop fusion | bytes 8388612 | tf_op jit(solution)/shard_map/dynamic_slice | solution.py:117
  153.9 65.8 %all-gather.12.cloned.1.call-done = bf16[2048,2048]{1,0:T(8,128)(2,1)} async-done(((bf16[2048,256]{1,0:T(8,128)(2,1)}), bf16[2048,2048]{1,0:T(8,128)(2,1)}) %all-gather.12.cloned.1.call-update) | async-done | bytes 8388624 | tf_op jit(solution)/shard_map/all_gather | solution.py:142
  219.7 4.8 %constant_dynamic-slice_fusion.3 = bf16[1024,2048]{1,0:T(8,128)(2,1)} fusion(bf16[2048,2048]{1,0:T(8,128)(2,1)} %all-gather.12.cloned.1.call-done, s32[]{:T(128)S(6)} %select_n.86), kind=kLoop, calls=%fused_computation.53 | loop fusion | bytes 8388612 | tf_op jit(solution)/shard_map/dynamic_slice | solution.py:117
  226.4 19.3 %collective-permute-done.1 = bf16[1024,2048]{1,0:T(8,128)(2,1)} collective-permute-done((bf16[1024,2048]{1,0:T(8,128)(2,1)}, bf16[1024,2048]{1,0:T(8,128)(2,1)}, u32[]{:S(2)}, u32[]{:S(2)}) %collective-permute-start.1) | collective-permute-done | bytes 4194336 | tf_op jit(solution)/shard_map/ppermute | solution.py:118
  245.7 2.7 collective-permute-start.2
  248.4 7.6 %fusion.36 = f32[512,2048]{1,0:T(8,128)S(1)} fusion(bf16[512,2048]{0,1:T(8,128)(2,1)} %bitcast.31, bf16[2048,2048]{1,0:T(8,128)(2,1)} %all-gather.8.cloned.1.call-done), kind=kOutput, calls=%fused_computation.75 | convolution fusion | flops 4294967296 | bytes 14680064 | tf_op jit(solution)/shard_map/dot_general | solution.py:171
  256.0 79.6 %collective-permute-done.7 = bf16[1024,2048]{1,0:T(8,128)(2,1)} collective-permute-done((bf16[1024,2048]{1,0:T(8,128)(2,1)}, bf16[1024,2048]{1,0:T(8,128)(2,1)}, u32[]{:S(2)}, u32[]{:S(2)}) %collective-permute-start.7) | collective-permute-done | bytes 4194336 | tf_op jit(solution)/shard_map/ppermute | solution.py:118
  335.6 1.5 collective-permute-start.8
  337.1 4.6 fusion.6
  341.8 4.9 %add_convert_fusion = bf16[512,2048]{1,0:T(8,128)(2,1)S(1)} fusion(f32[512,2048]{1,0:T(8,128)S(1)} %fusion.36, f32[512,2048]{1,0:T(8,128)S(1)} %fusion.6, bf16[1024,2048]{1,0:T(8,128)(2,1)} %collective-permute-done.2, bf16[512,2048]{0,1:T(8,128)(2,1)S(1)} %bitcast.29, s32[]{:T(128)S(6)} %select_n.87), kind=kOutput, calls=%fused_computation.4 | convolution fusion | flops 2150629376 | bytes 15728644 | tf_op jit(solution)/shard_map/dot_general | solution.py:173
  346.9 2.2 copy-done.3
  349.1 27.5 %shard_map.64 = bf16[512,1024]{1,0:T(8,128)(2,1)S(1)} custom-call(s32[1]{0:T(128)} %bitcast.start_ref, bf16[512,1024]{1,0:T(8,128)(2,1)S(1)} %slice.36.q_ref, bf16[4096,512]{1,0:T(8,128)(2,1)S(1)} %copy-done.3, bf16[4096,512]{1,0:T(8,128)(2,1)S(1)} %copy-done.3), custom_call_target="tpu_custom_call" | custom-call | flops 17179869184 | bytes 6291456 | tf_op jit(solution)/shard_map/pallas_call | solution.py:86
  376.7 2.2 copy-done.2
  378.8 19.2 %shard_map.65 = bf16[256,1024]{1,0:T(8,128)(2,1)S(1)} custom-call(s32[1]{0:T(128)} %bitcast.start_ref, bf16[256,1024]{1,0:T(8,128)(2,1)S(1)} %get-tuple-element.7.q_ref, bf16[4096,512]{1,0:T(8,128)(2,1)S(1)} %copy-done.2, bf16[4096,512]{1,0:T(8,128)(2,1)S(1)} %copy-done.2), custom_call_target="tpu_custom_call" | custom-call | flops 8589934592 | bytes 5242880 | tf_op jit(solution)/shard_map/pallas_call | solution.py:86
  398.0 5.7 %convolution_convert_fusion.1 = bf16[256,2048]{1,0:T(8,128)(2,1)S(1)} fusion(bf16[2048,2048]{1,0:T(8,128)(2,1)} %all-gather.12.cloned.1.call-done, bf16[256,1024]{1,0:T(8,128)(2,1)S(1)} %shard_map.65, bf16[256,1024]{1,0:T(8,128)(2,1)S(1)} %get-tuple-element.9), kind=kOutput, calls=%fused_computation.10 | convolution fusion | flops 2150105088 | bytes 10485760 | tf_op jit(solution)/shard_map/dot_general | solution.py:228
  403.8 1.3 collective-permute-start.6
  405.1 3.5 fusion.15
  408.6 3.7 fusion
  412.6 18.9 %shard_map.66 = bf16[256,1024]{1,0:T(8,128)(2,1)S(1)} custom-call(s32[1]{0:T(128)} %bitcast.6.start_ref, bf16[256,1024]{1,0:T(8,128)(2,1)S(1)} %get-tuple-element.8.q_ref, bf16[4096,512]{1,0:T(8,128)(2,1)S(1)} %copy-done.2, bf16[4096,512]{1,0:T(8,128)(2,1)S(1)} %copy-done.2), custom_call_target="tpu_custom_call" | custom-call | flops 8589934592 | bytes 5242880 | tf_op jit(solution)/shard_map/pallas_call | solution.py:86
  431.5 2.4 convolution_convert_fusion
  434.9 1.2 collective-permute-start.10
  436.1 3.5 fusion.10
  439.6 3.5 fusion.1
  446.3 1.6 copy.13
  447.9 1.8 select_n.91
  449.7 1.4 add_convert_fusion.3
  451.1 1.2 stack_reshape.18
  452.3 7.1 %collective-permute-done.11 = bf16[256,1024]{1,0:T(8,128)(2,1)} collective-permute-done((bf16[256,1024]{1,0:T(8,128)(2,1)}, bf16[256,1024]{1,0:T(8,128)(2,1)}, u32[]{:S(2)}, u32[]{:S(2)}) %collective-permute-start.11) | collective-permute-done | bytes 524320 | tf_op jit(solution)/shard_map/ppermute | solution.py:203
  459.4 1.2 add_convert_fusion.2
  461.0 2.4 maximum_select_fusion.3
  463.4 1.6 copy.14
  465.0 1.6 select_n.93
  466.6 3.1 maximum_bitcast_fusion
  (64 shorter events, 10.4 us)
Async XLA Ops:
  6.5 2.1 copy-start
  6.5 48.7 %all-gather.10.cloned.1.call-start = ((), (), s32[]{:S(2)}) async-start(), calls=%async_computation.1 | async-start | bytes 4718592 | tf_op jit(solution)/shard_map/all_gather | solution.py:136
  8.6 140.1 %all-gather.8.cloned.1.call-start = ((), (), s32[]{:S(2)}) async-start(), calls=%async_computation | async-start | bytes 9437184 | tf_op jit(solution)/shard_map/all_gather | solution.py:139
  9.8 210.0 %all-gather.12.cloned.1.call-start = ((), (), s32[]{:S(2)}) async-start(), calls=%async_computation.2 | async-start | bytes 9437184 | tf_op jit(solution)/shard_map/all_gather | solution.py:142
  12.1 334.7 %all-gather.14.cloned.1.call-start = ((), (), s32[]{:S(2)}) async-start(), calls=%async_computation.3 | async-start | bytes 4718592 | tf_op jit(solution)/shard_map/all_gather | solution.py:189
  12.2 47.6 %copy-start.7 = (f32[4096]{0:T(1024)S(1)}, f32[4096]{0:T(1024)}, u32[]{:S(2)}) copy-start(f32[4096]{0:T(1024)} %param.7) | copy-start | bytes 49156
  58.4 47.3 %collective-permute-start.3 = (bf16[1024,1024]{1,0:T(8,128)(2,1)}, bf16[1024,1024]{1,0:T(8,128)(2,1)}, u32[]{:S(2)}, u32[]{:S(2)}) collective-permute-start(bf16[1024,1024]{1,0:T(8,128)(2,1)} %constant_dynamic-slice_fusion.6), channel_id=1, source_target_pairs={{0,16},{16,0},{1,17},{17,1},{2,18},{18,2},{3,19},{19,3},{4,20},{20... | collective-permute-start | bytes 6291464 | tf_op jit(solution)/shard_map/ppermute | solution.py:118
  58.6 48.1 %collective-permute-start = (bf16[512,2048]{0,1:T(8,128)(2,1)S(1)}, bf16[512,2048]{0,1:T(8,128)(2,1)}, u32[]{:S(2)}, u32[]{:S(2)}) collective-permute-start(bf16[512,2048]{0,1:T(8,128)(2,1)S(1)} %bitcast.23), channel_id=1, source_target_pairs={{0,1},{1,0},{2,3},{3,2},{4,5},{5,4},{6,7},{7,6},{8,9},{9,8},{10,11... | collective-permute-start | bytes 6291464 | tf_op jit(solution)/shard_map/ppermute | solution.py:148
  105.6 15.6 %collective-permute-start.4 = (bf16[1024,1024]{1,0:T(8,128)(2,1)}, bf16[1024,1024]{1,0:T(8,128)(2,1)S(1)}, u32[]{:S(2)}, u32[]{:S(2)}) collective-permute-start(bf16[1024,1024]{1,0:T(8,128)(2,1)} %collective-permute-done.3), channel_id=1, source_target_pairs={{0,2},{2,0},{4,6},{6,4},{8,10},{10,8},{12,14},{14,12},{1,3},{3,1},... | collective-permute-start | bytes 6291464 | tf_op jit(solution)/shard_map/ppermute | solution.py:18
  113.0 3.0 copy-start.5
  113.3 5.0 %copy-start.4 = (bf16[512,8,1,256]{0,3,2,1:T(8,128)(2,1)}, bf16[512,8,1,256]{0,3,2,1:T(8,128)(2,1)S(1)}, u32[]{:S(2)}) copy-start(bf16[512,8,1,256]{0,3,2,1:T(8,128)(2,1)S(1)} %get-tuple-element.6) | copy-start | bytes 6291460
  122.6 24.8 %collective-permute-start.5 = (bf16[512,1024]{1,0:T(8,128)(2,1)S(1)}, bf16[512,1024]{1,0:T(8,128)(2,1)S(1)}, u32[]{:S(2)}, u32[]{:S(2)}) collective-permute-start(bf16[512,1024]{1,0:T(8,128)(2,1)S(1)} %add_convert_fusion.1), channel_id=1, source_target_pairs={{0,16},{16,0},{1,17},{17,1},{2,18},{18,2},{3,19},{19,3},{4,20},{20... | collective-permute-start | bytes 3145736 | tf_op jit(solution)/shard_map/ppermute | solution.py:177
  148.4 228.3 %all-gather.16.cloned.1.call-start = ((), (), s32[]{:S(2)}) async-start(), calls=%async_computation.4 | async-start | bytes 4718592 | tf_op jit(solution)/shard_map/all_gather | solution.py:189
  153.9 91.8 %collective-permute-start.1 = (bf16[1024,2048]{1,0:T(8,128)(2,1)}, bf16[1024,2048]{1,0:T(8,128)(2,1)}, u32[]{:S(2)}, u32[]{:S(2)}) collective-permute-start(bf16[1024,2048]{1,0:T(8,128)(2,1)} %constant_dynamic-slice_fusion.7), channel_id=1, source_target_pairs={{0,16},{16,0},{1,17},{17,1},{2,18},{18,2},{3,19},{19,3},{4,20},{20... | collective-permute-start | bytes 12582920 | tf_op jit(solution)/shard_map/ppermute | solution.py:118
  224.5 111.0 %collective-permute-start.7 = (bf16[1024,2048]{1,0:T(8,128)(2,1)}, bf16[1024,2048]{1,0:T(8,128)(2,1)}, u32[]{:S(2)}, u32[]{:S(2)}) collective-permute-start(bf16[1024,2048]{1,0:T(8,128)(2,1)} %constant_dynamic-slice_fusion.3), channel_id=1, source_target_pairs={{0,16},{16,0},{1,17},{17,1},{2,18},{18,2},{3,19},{19,3},{4,20},{20... | collective-permute-start | bytes 12582920 | tf_op jit(solution)/shard_map/ppermute | solution.py:118
  245.7 96.1 %collective-permute-start.2 = (bf16[1024,2048]{1,0:T(8,128)(2,1)}, bf16[1024,2048]{1,0:T(8,128)(2,1)}, u32[]{:S(2)}, u32[]{:S(2)}) collective-permute-start(bf16[1024,2048]{1,0:T(8,128)(2,1)} %collective-permute-done.1), channel_id=1, source_target_pairs={{0,2},{2,0},{4,6},{6,4},{8,10},{10,8},{12,14},{14,12},{1,3},{3,1},... | collective-permute-start | bytes 12582920 | tf_op jit(solution)/shard_map/ppermute | solution.py:18
  335.6 73.0 %collective-permute-start.8 = (bf16[1024,2048]{1,0:T(8,128)(2,1)}, bf16[1024,2048]{1,0:T(8,128)(2,1)}, u32[]{:S(2)}, u32[]{:S(2)}) collective-permute-start(bf16[1024,2048]{1,0:T(8,128)(2,1)} %collective-permute-done.7), channel_id=1, source_target_pairs={{0,2},{2,0},{4,6},{6,4},{8,10},{10,8},{12,14},{14,12},{1,3},{3,1},... | collective-permute-start | bytes 12582920 | tf_op jit(solution)/shard_map/ppermute | solution.py:18
  346.9 2.2 copy-start.3
  376.7 2.2 copy-start.2
  403.8 40.5 %collective-permute-start.6 = (bf16[256,1024]{1,0:T(8,128)(2,1)S(1)}, bf16[256,1024]{1,0:T(8,128)(2,1)S(1)}, u32[]{:S(2)}, u32[]{:S(2)}) collective-permute-start(bf16[256,1024]{1,0:T(8,128)(2,1)S(1)} %constant_dynamic-slice_fusion.4), channel_id=1, source_target_pairs={{0,1},{1,0},{2,3},{3,2},{4,5},{5,4},{6,7},{7,6},{8,9},{9,8},{10,11... | collective-permute-start | bytes 1572872 | tf_op jit(solution)/shard_map/ppermute | solution.py:203
  408.6 23.0 %slice-start = ((s8[8388608]{0:T(1024)(128)(4,1)}), s8[4194304]{0:T(1024)(128)(4,1)S(1)}, s32[]{:S(2)}) async-start(s8[8388608]{0:T(1024)(128)(4,1)} %bitcast.32), calls=%async_computation.5 | async-start | bytes 8388608
  412.3 32.2 %collective-permute-start.9 = (bf16[256,1024]{1,0:T(8,128)(2,1)S(1)}, bf16[256,1024]{1,0:T(8,128)(2,1)S(1)}, u32[]{:S(2)}, u32[]{:S(2)}) collective-permute-start(bf16[256,1024]{1,0:T(8,128)(2,1)S(1)} %constant_dynamic-slice_fusion.2), channel_id=1, source_target_pairs={{0,1},{1,0},{2,3},{3,2},{4,5},{5,4},{6,7},{7,6},{8,9},{9,8},{10,11... | collective-permute-start | bytes 1572872 | tf_op jit(solution)/shard_map/ppermute | solution.py:203
  412.6 18.9 %slice-start.1 = ((s8[8388608]{0:T(1024)(128)(4,1)}), s8[4194304]{0:T(1024)(128)(4,1)S(1)}, s32[]{:S(2)}) async-start(s8[8388608]{0:T(1024)(128)(4,1)} %bitcast.32), calls=%async_computation.6 | async-start | bytes 8388608
  434.0 5.7 %copy-start.6 = (bf16[256,2048]{1,0:T(8,128)(2,1)}, bf16[256,2048]{1,0:T(8,128)(2,1)S(1)}, u32[]{:S(2)}) copy-start(bf16[256,2048]{1,0:T(8,128)(2,1)S(1)} %convolution_convert_fusion) | copy-start | bytes 3145732
  434.9 14.8 %collective-permute-start.10 = (bf16[256,1024]{1,0:T(8,128)(2,1)}, bf16[256,1024]{1,0:T(8,128)(2,1)}, u32[]{:S(2)}, u32[]{:S(2)}) collective-permute-start(bf16[256,1024]{1,0:T(8,128)(2,1)} %constant_dynamic-slice_fusion.1), channel_id=1, source_target_pairs={{0,1},{1,0},{2,3},{3,2},{4,5},{5,4},{6,7},{7,6},{8,9},{9,8},{10,11... | collective-permute-start | bytes 1572872 | tf_op jit(solution)/shard_map/ppermute | solution.py:203
  444.0 15.4 %collective-permute-start.11 = (bf16[256,1024]{1,0:T(8,128)(2,1)}, bf16[256,1024]{1,0:T(8,128)(2,1)}, u32[]{:S(2)}, u32[]{:S(2)}) collective-permute-start(bf16[256,1024]{1,0:T(8,128)(2,1)} %constant_dynamic-slice_fusion), channel_id=1, source_target_pairs={{0,1},{1,0},{2,3},{3,2},{4,5},{5,4},{6,7},{7,6},{8,9},{9,8},{10,11... | collective-permute-start | bytes 1572872 | tf_op jit(solution)/shard_map/ppermute | solution.py:203
  461.0 8.7 %copy-start.1 = (bf16[512,2048]{1,0:T(8,128)(2,1)S(1)}, bf16[512,2048]{1,0:T(8,128)(2,1)}, u32[]{:S(2)}) copy-start(bf16[512,2048]{1,0:T(8,128)(2,1)} %param.8) | copy-start | bytes 6291460
Sparse Core Ops, SparseCore 0:
  9.0 46.2 all-gather.9
  56.9 80.4 all-gather.7
  139.0 80.6 all-gather.11
  221.2 45.9 all-gather.13
  268.6 45.8 all-gather.15

commit v3 on v2

--- a/solution.py
+++ b/solution.py
@@ -112,12 +112,14 @@
     )(start.reshape(1), queries, keys_values, keys_values)
 
 
-def y_share(mine, core):
+def y_share(mine, core, after=None):
     depth = mine.shape[0] // 2
     part = lax.dynamic_slice_in_dim(mine, core * depth, depth, 0)
     near = lax.ppermute(part, "stream", [(0, 1), (1, 0)])
-    far = swap_pairs(near, "seq")
-    return near, far
+    if after is None:
+        return near, swap_pairs(near, "seq")
+    near, after = lax.optimization_barrier((near, after))
+    return near, swap_pairs(near, "seq"), after
 
 
 def body(hidden, norm_gain, query_weight, key_weight, value_projection_weight, out_weight):
@@ -189,7 +191,7 @@
             lax.all_gather(columns.reshape(windows, frame_count, 2 * step), "seq", axis=1, tiled=True)
         )
     queries = project(query_mine, *y_share(query_mine, core)).reshape(windows, frame_count, -1)
-    out_near, out_far = y_share(out_mine, core)
+    out_near = out_far = None
     width = out_weight.shape[0] // 2
 
     repeat = query_weight.shape[1] // key_weight.shape[1]
@@ -226,6 +228,8 @@
             )
             attended = jnp.concatenate([done[low:high] for done in early] + [final], axis=1)
             share_mine = jnp.dot(attended, out_mine, preferred_element_type=jnp.float32)
+            if out_near is None:
+                out_near, out_far, attended = y_share(out_mine, core, attended)
             attended_near = lax.dynamic_slice_in_dim(attended, core * width, width, 1)
             attended_far = lax.dynamic_slice_in_dim(attended, (1 - core) * width, width, 1)
             share_other = jnp.dot(attended_near, out_near, preferred_element_type=jnp.float32)

time: 483 us -> 434 us (0.90)
  waiting for transfers between devices: 282 us -> 235 us
    all_gather x1, waiting for transfers between devices: 65.8 us -> 0.01 us  [body(): lax.all_gather(lax.dynamic_slice_in_dim(out_weight, stream * out_half, ou...]
    all_gather x2, waiting for transfers between devices: 0.04 us -> 15.5 us  [body(): lax.all_gather(columns.reshape(windows, frame_count, 2 * step), 'seq', ax...]
    unnamed x21 -> x27, local copies, waits for them, and re-layouts: 9.93 us -> 10.2 us
  transfers between devices with their start and end apart: 17 -> 17, of which waited for: 7 -> 8; matrix products, arithmetic and copies ran while one was open for 18% -> 20% of each run, Pallas kernels for 14% -> 15%
where the time goes in v3:
time: 434 us; the launch traced here: 427 us
  waiting for transfers between devices  235 us (54%)
  Pallas kernels  65.5 us (15%)
  matrix products  45.4 us (10%)
  local copies, waits for them, and re-layouts  38.4 us (9%)
  other arithmetic  20.1 us (5%)
  between operations  13.8 us (3%)
  starting transfers between devices  8.7 us (2%)
    ppermute x3, waiting for transfers between devices, y_share(): near = lax.ppermute(part, 'stream', [(0, 1), (1, 0)])  145 us
    pallas_call x3, Pallas kernels, attend(): pl.pallas_call(functools.partial(attend_kernel, repeat), out_shape=jax.Sh...  65.5 us
    all_gather x1, waiting for transfers between devices, body(): lax.all_gather(lax.dynamic_slice_in_dim(kv_weight, stream * depth, depth,...  40.2 us
    ppermute x1, waiting for transfers between devices, body(): partner = lax.ppermute(keys_values, 'stream', [(0, 1), (1, 0)])  24.4 us
    all_gather x2, waiting for transfers between devices, body(): lax.all_gather(columns.reshape(windows, frame_count, 2 * step), 'seq', ax...  15.5 us
    dynamic_slice x3, local copies, waits for them, and re-layouts, y_share(): part = lax.dynamic_slice_in_dim(mine, core * depth, depth, 0)  13.4 us
    ppermute x4, waiting for transfers between devices, scattered(): came = lax.ppermute(away, 'tensor', [(0, 1), (1, 0)])  10.3 us
    unnamed x27, local copies, waits for them, and re-layouts  10.2 us
  transfers between devices with their start and end apart: 17, of which 8 were waited for; matrix products, arithmetic and copies ran while one was open for 20% of the time, Pallas kernels for 15%

profile of v3, /device:TPU:29, one launch (start us, length us, event | category | flops | bytes accessed | tf_op | source)
XLA Modules:
  0.0 427.0 jit_solution(7963801564547293652)
XLA Ops:
  6.5 2.0 fusion.8
  8.6 1.1 constant_dynamic-slice_fusion.9
  9.8 2.3 constant_dynamic-slice_fusion.5
  12.2 2.9 copy.11
  15.1 40.2 %all-gather.10.cloned.1.call-done = bf16[2048,1024]{1,0:T(8,128)(2,1)} async-done(((bf16[256,1024]{1,0:T(8,128)(2,1)}), bf16[2048,1024]{1,0:T(8,128)(2,1)}) %all-gather.10.cloned.1.call-update) | async-done | bytes 4194320 | tf_op jit(solution)/shard_map/all_gather | solution.py:138
  55.3 3.1 constant_dynamic-slice_fusion.6
  58.6 1.2 collective-permute-start
  59.8 45.8 %collective-permute-done.3 = bf16[1024,1024]{1,0:T(8,128)(2,1)} collective-permute-done((bf16[1024,1024]{1,0:T(8,128)(2,1)}, bf16[1024,1024]{1,0:T(8,128)(2,1)}, u32[]{:S(2)}, u32[]{:S(2)}) %collective-permute-start.3) | collective-permute-done | bytes 2097184 | tf_op jit(solution)/shard_map/ppermute | solution.py:118
  106.7 3.1 multiply_reduce_fusion
  109.8 3.2 multiply_convert_fusion
  113.3 2.7 copy-done.7
  116.0 2.3 fusion.32
  118.3 2.9 fusion.4
  121.2 1.4 add_convert_fusion.1
  123.0 24.4 %collective-permute-done.5 = bf16[512,1024]{1,0:T(8,128)(2,1)S(1)} collective-permute-done((bf16[512,1024]{1,0:T(8,128)(2,1)S(1)}, bf16[512,1024]{1,0:T(8,128)(2,1)S(1)}, u32[]{:S(2)}, u32[]{:S(2)}) %collective-permute-start.5) | collective-permute-done | bytes 1048608 | tf_op jit(solution)/shard_map/ppermute | solution.py:179
  148.6 5.3 %constant_dynamic-slice_fusion.7 = bf16[1024,2048]{1,0:T(8,128)(2,1)} fusion(bf16[2048,2048]{1,0:T(8,128)(2,1)} %all-gather.8.cloned.1.call-done, s32[]{:T(128)S(6)} %select_n.86), kind=kLoop, calls=%fused_computation.56 | loop fusion | bytes 8388612 | tf_op jit(solution)/shard_map/dynamic_slice | solution.py:117
  154.8 90.9 %collective-permute-done.1 = bf16[1024,2048]{1,0:T(8,128)(2,1)} collective-permute-done((bf16[1024,2048]{1,0:T(8,128)(2,1)}, bf16[1024,2048]{1,0:T(8,128)(2,1)}, u32[]{:S(2)}, u32[]{:S(2)}) %collective-permute-start.1) | collective-permute-done | bytes 4194336 | tf_op jit(solution)/shard_map/ppermute | solution.py:118
  245.7 1.5 collective-permute-start.2
  247.2 5.1 %constant_dynamic-slice_fusion.3 = bf16[1024,2048]{1,0:T(8,128)(2,1)} fusion(bf16[2048,2048]{1,0:T(8,128)(2,1)} %all-gather.12.cloned.1.call-done, s32[]{:T(128)S(6)} %select_n.86), kind=kLoop, calls=%fused_computation.50 | loop fusion | bytes 8388612 | tf_op jit(solution)/shard_map/dynamic_slice | solution.py:117
  252.3 7.2 %fusion.31 = f32[512,2048]{1,0:T(8,128)S(1)} fusion(bf16[512,2048]{0,1:T(8,128)(2,1)S(1)} %bitcast.31, bf16[2048,2048]{1,0:T(8,128)(2,1)} %all-gather.8.cloned.1.call-done), kind=kOutput, calls=%fused_computation.68 | convolution fusion | flops 4294967296 | bytes 14680064 | tf_op jit(solution)/shard_map/dot_general | solution.py:173
  259.5 4.7 %fusion.6 = f32[512,2048]{1,0:T(8,128)S(1)} fusion(bf16[1024,2048]{1,0:T(8,128)(2,1)} %collective-permute-done.1, bf16[512,2048]{0,1:T(8,128)(2,1)S(1)} %bitcast.28, s32[]{:T(128)S(6)} %select_n.86), kind=kOutput, calls=%fused_computation.31 | convolution fusion | flops 2147483648 | bytes 9437188 | tf_op jit(solution)/shard_map/dot_general | solution.py:174
  264.1 5.0 %add_convert_fusion = bf16[512,2048]{1,0:T(8,128)(2,1)S(1)} fusion(f32[512,2048]{1,0:T(8,128)S(1)} %fusion.31, f32[512,2048]{1,0:T(8,128)S(1)} %fusion.6, bf16[1024,2048]{1,0:T(8,128)(2,1)} %collective-permute-done.2, bf16[512,2048]{0,1:T(8,128)(2,1)S(1)} %bitcast.29, s32[]{:T(128)S(6)} %select_n.87), kind=kOutput, calls=%fused_computation.4 | convolution fusion | flops 2150629376 | bytes 15728644 | tf_op jit(solution)/shard_map/dot_general | solution.py:175
  269.3 2.2 copy-done.4
  271.5 27.5 %shard_map.64 = bf16[512,1024]{1,0:T(8,128)(2,1)S(1)} custom-call(s32[1]{0:T(128)} %bitcast.start_ref, bf16[512,1024]{1,0:T(8,128)(2,1)S(1)} %slice.36.q_ref, bf16[4096,512]{1,0:T(8,128)(2,1)S(1)} %copy-done.4, bf16[4096,512]{1,0:T(8,128)(2,1)S(1)} %copy-done.4), custom_call_target="tpu_custom_call" | custom-call | flops 17179869184 | bytes 6291456 | tf_op jit(solution)/shard_map/pallas_call | solution.py:86
  299.1 15.5 %all-gather.16.cloned.1.call-done.k_ref.v_ref = bf16[4096,512]{1,0:T(8,128)(2,1)} async-done(((bf16[512,512]{1,0:T(8,128)(2,1)}), bf16[4096,512]{1,0:T(8,128)(2,1)}) %all-gather.16.cloned.1.call-update) | async-done | bytes 4194320 | tf_op jit(solution)/shard_map/all_gather | solution.py:191
  314.5 2.2 copy-done.2
  316.7 19.2 %shard_map.65 = bf16[256,1024]{1,0:T(8,128)(2,1)S(1)} custom-call(s32[1]{0:T(128)} %bitcast.start_ref, bf16[256,1024]{1,0:T(8,128)(2,1)S(1)} %get-tuple-element.12.q_ref, bf16[4096,512]{1,0:T(8,128)(2,1)S(1)} %copy-done.2, bf16[4096,512]{1,0:T(8,128)(2,1)S(1)} %copy-done.2), custom_call_target="tpu_custom_call" | custom-call | flops 8589934592 | bytes 5242880 | tf_op jit(solution)/shard_map/pallas_call | solution.py:86
  337.0 7.9 %collective-permute-done.7 = bf16[1024,2048]{1,0:T(8,128)(2,1)} collective-permute-done((bf16[1024,2048]{1,0:T(8,128)(2,1)}, bf16[1024,2048]{1,0:T(8,128)(2,1)}, u32[]{:S(2)}, u32[]{:S(2)}) %collective-permute-start.7) | collective-permute-done | bytes 4194336 | tf_op jit(solution)/shard_map/ppermute | solution.py:118
  345.6 5.9 %convolution_convert_fusion.1 = bf16[256,2048]{1,0:T(8,128)(2,1)S(1)} fusion(bf16[2048,2048]{1,0:T(8,128)(2,1)} %all-gather.12.cloned.1.call-done, bf16[256,1024]{1,0:T(8,128)(2,1)S(1)} %shard_map.65, bf16[256,1024]{1,0:T(8,128)(2,1)S(1)} %get-tuple-element.14), kind=kOutput, calls=%fused_computation.10 | convolution fusion | flops 2150105088 | bytes 10485760 | tf_op jit(solution)/shard_map/dot_general | solution.py:230
  351.5 1.3 collective-permute-start.6
  352.8 18.9 %shard_map.66 = bf16[256,1024]{1,0:T(8,128)(2,1)S(1)} custom-call(s32[1]{0:T(128)} %bitcast.6.start_ref, bf16[256,1024]{1,0:T(8,128)(2,1)S(1)} %get-tuple-element.11.q_ref, bf16[4096,512]{1,0:T(8,128)(2,1)S(1)} %copy-done.3, bf16[4096,512]{1,0:T(8,128)(2,1)S(1)} %copy-done.3), custom_call_target="tpu_custom_call" | custom-call | flops 8589934592 | bytes 5242880 | tf_op jit(solution)/shard_map/pallas_call | solution.py:86
  371.7 2.3 convolution_convert_fusion
  374.7 3.4 fusion.14
  378.1 3.5 fusion
  382.7 1.2 collective-permute-start.9
  383.9 3.5 fusion.12
  387.4 3.5 fusion.1
  392.6 1.2 stack_reshape.18
  393.8 4.8 %collective-permute-done.9 = bf16[256,1024]{1,0:T(8,128)(2,1)S(1)} collective-permute-done((bf16[256,1024]{1,0:T(8,128)(2,1)}, bf16[256,1024]{1,0:T(8,128)(2,1)S(1)}, u32[]{:S(2)}, u32[]{:S(2)}) %collective-permute-start.9) | collective-permute-done | bytes 524320 | tf_op jit(solution)/shard_map/ppermute | solution.py:205
  398.6 1.2 add_convert_fusion.4
  401.0 1.6 copy.13
  402.6 1.8 select_n.91
  404.4 5.5 %collective-permute-done.11 = bf16[256,1024]{1,0:T(8,128)(2,1)} collective-permute-done((bf16[256,1024]{1,0:T(8,128)(2,1)}, bf16[256,1024]{1,0:T(8,128)(2,1)}, u32[]{:S(2)}, u32[]{:S(2)}) %collective-permute-start.11) | collective-permute-done | bytes 524320 | tf_op jit(solution)/shard_map/ppermute | solution.py:205
  409.9 1.2 add_convert_fusion.2
  411.6 2.4 maximum_select_fusion.3
  413.9 1.6 copy.14
  415.6 1.6 select_n.93
  417.2 3.1 maximum_bitcast_fusion
  (71 shorter events, 11.5 us)
Async XLA Ops:
  6.5 2.1 copy-start
  6.5 48.7 %all-gather.10.cloned.1.call-start = ((), (), s32[]{:S(2)}) async-start(), calls=%async_computation.1 | async-start | bytes 4718592 | tf_op jit(solution)/shard_map/all_gather | solution.py:138
  8.6 140.0 %all-gather.8.cloned.1.call-start = ((), (), s32[]{:S(2)}) async-start(), calls=%async_computation | async-start | bytes 9437184 | tf_op jit(solution)/shard_map/all_gather | solution.py:141
  9.8 237.5 %all-gather.12.cloned.1.call-start = ((), (), s32[]{:S(2)}) async-start(), calls=%async_computation.2 | async-start | bytes 9437184 | tf_op jit(solution)/shard_map/all_gather | solution.py:144
  12.1 257.2 %all-gather.14.cloned.1.call-start = ((), (), s32[]{:S(2)}) async-start(), calls=%async_computation.3 | async-start | bytes 4718592 | tf_op jit(solution)/shard_map/all_gather | solution.py:191
  12.2 47.6 %copy-start.10 = (f32[4096]{0:T(1024)S(1)}, f32[4096]{0:T(1024)}, u32[]{:S(2)}) copy-start(f32[4096]{0:T(1024)} %param.7) | copy-start | bytes 49156
  58.4 47.3 %collective-permute-start.3 = (bf16[1024,1024]{1,0:T(8,128)(2,1)}, bf16[1024,1024]{1,0:T(8,128)(2,1)}, u32[]{:S(2)}, u32[]{:S(2)}) collective-permute-start(bf16[1024,1024]{1,0:T(8,128)(2,1)} %constant_dynamic-slice_fusion.6), channel_id=1, source_target_pairs={{0,16},{16,0},{1,17},{17,1},{2,18},{18,2},{3,19},{19,3},{4,20},{20... | collective-permute-start | bytes 6291464 | tf_op jit(solution)/shard_map/ppermute | solution.py:118
  58.6 48.1 %collective-permute-start = (bf16[512,2048]{0,1:T(8,128)(2,1)S(1)}, bf16[512,2048]{0,1:T(8,128)(2,1)}, u32[]{:S(2)}, u32[]{:S(2)}) collective-permute-start(bf16[512,2048]{0,1:T(8,128)(2,1)S(1)} %bitcast.23), channel_id=1, source_target_pairs={{0,1},{1,0},{2,3},{3,2},{4,5},{5,4},{6,7},{7,6},{8,9},{9,8},{10,11... | collective-permute-start | bytes 6291464 | tf_op jit(solution)/shard_map/ppermute | solution.py:150
  105.6 15.6 %collective-permute-start.4 = (bf16[1024,1024]{1,0:T(8,128)(2,1)}, bf16[1024,1024]{1,0:T(8,128)(2,1)S(1)}, u32[]{:S(2)}, u32[]{:S(2)}) collective-permute-start(bf16[1024,1024]{1,0:T(8,128)(2,1)} %collective-permute-done.3), channel_id=1, source_target_pairs={{0,2},{2,0},{4,6},{6,4},{8,10},{10,8},{12,14},{14,12},{1,3},{3,1},... | collective-permute-start | bytes 6291464 | tf_op jit(solution)/shard_map/ppermute | solution.py:18
  113.0 3.0 copy-start.7
  113.3 5.0 %copy-start.5 = (bf16[512,8,1,256]{0,3,2,1:T(8,128)(2,1)}, bf16[512,8,1,256]{0,3,2,1:T(8,128)(2,1)S(1)}, u32[]{:S(2)}) copy-start(bf16[512,8,1,256]{0,3,2,1:T(8,128)(2,1)S(1)} %get-tuple-element.10) | copy-start | bytes 6291460
  122.6 24.8 %collective-permute-start.5 = (bf16[512,1024]{1,0:T(8,128)(2,1)S(1)}, bf16[512,1024]{1,0:T(8,128)(2,1)S(1)}, u32[]{:S(2)}, u32[]{:S(2)}) collective-permute-start(bf16[512,1024]{1,0:T(8,128)(2,1)S(1)} %add_convert_fusion.1), channel_id=1, source_target_pairs={{0,16},{16,0},{1,17},{17,1},{2,18},{18,2},{3,19},{19,3},{4,20},{20... | collective-permute-start | bytes 3145736 | tf_op jit(solution)/shard_map/ppermute | solution.py:179
  148.4 166.2 %all-gather.16.cloned.1.call-start = ((), (), s32[]{:S(2)}) async-start(), calls=%async_computation.4 | async-start | bytes 4718592 | tf_op jit(solution)/shard_map/all_gather | solution.py:191
  153.9 91.8 %collective-permute-start.1 = (bf16[1024,2048]{1,0:T(8,128)(2,1)}, bf16[1024,2048]{1,0:T(8,128)(2,1)}, u32[]{:S(2)}, u32[]{:S(2)}) collective-permute-start(bf16[1024,2048]{1,0:T(8,128)(2,1)} %constant_dynamic-slice_fusion.7), channel_id=1, source_target_pairs={{0,16},{16,0},{1,17},{17,1},{2,18},{18,2},{3,19},{19,3},{4,20},{20... | collective-permute-start | bytes 12582920 | tf_op jit(solution)/shard_map/ppermute | solution.py:118
  245.7 18.4 %collective-permute-start.2 = (bf16[1024,2048]{1,0:T(8,128)(2,1)}, bf16[1024,2048]{1,0:T(8,128)(2,1)}, u32[]{:S(2)}, u32[]{:S(2)}) collective-permute-start(bf16[1024,2048]{1,0:T(8,128)(2,1)} %collective-permute-done.1), channel_id=1, source_target_pairs={{0,2},{2,0},{4,6},{6,4},{8,10},{10,8},{12,14},{14,12},{1,3},{3,1},... | collective-permute-start | bytes 12582920 | tf_op jit(solution)/shard_map/ppermute | solution.py:18
  247.2 5.1 %copy-start.6 = (bf16[512,8,1,256]{0,3,2,1:T(8,128)(2,1)S(1)}, bf16[512,8,1,256]{0,3,2,1:T(8,128)(2,1)}, u32[]{:S(2)}) copy-start(bf16[512,8,1,256]{0,3,2,1:T(8,128)(2,1)} %copy-done.5) | copy-start | bytes 6291460
  252.3 92.6 %collective-permute-start.7 = (bf16[1024,2048]{1,0:T(8,128)(2,1)}, bf16[1024,2048]{1,0:T(8,128)(2,1)}, u32[]{:S(2)}, u32[]{:S(2)}) collective-permute-start(bf16[1024,2048]{1,0:T(8,128)(2,1)} %constant_dynamic-slice_fusion.3), channel_id=1, source_target_pairs={{0,16},{16,0},{1,17},{17,1},{2,18},{18,2},{3,19},{19,3},{4,20},{20... | collective-permute-start | bytes 12582920 | tf_op jit(solution)/shard_map/ppermute | solution.py:118
  269.3 2.2 copy-start.4
  314.5 2.2 copy-start.2
  344.8 29.8 %collective-permute-start.8 = (bf16[1024,2048]{1,0:T(8,128)(2,1)}, bf16[1024,2048]{1,0:T(8,128)(2,1)}, u32[]{:S(2)}, u32[]{:S(2)}) collective-permute-start(bf16[1024,2048]{1,0:T(8,128)(2,1)} %collective-permute-done.7), channel_id=1, source_target_pairs={{0,2},{2,0},{4,6},{6,4},{8,10},{10,8},{12,14},{14,12},{1,3},{3,1},... | collective-permute-start | bytes 12582920 | tf_op jit(solution)/shard_map/ppermute | solution.py:18
  345.6 7.2 %copy-start.3 = (bf16[4096,512]{1,0:T(8,128)(2,1)S(1)}, bf16[4096,512]{1,0:T(8,128)(2,1)}, u32[]{:S(2)}) copy-start(bf16[4096,512]{1,0:T(8,128)(2,1)} %all-gather.16.cloned.1.call-done.k_ref.v_ref) | copy-start | bytes 12582916
  345.6 26.1 %slice-start = ((s8[8388608]{0:T(1024)(128)(4,1)}), s8[4194304]{0:T(1024)(128)(4,1)S(1)}, s32[]{:S(2)}) async-start(s8[8388608]{0:T(1024)(128)(4,1)} %bitcast.32), calls=%async_computation.5 | async-start | bytes 8388608
  351.5 22.9 %collective-permute-start.6 = (bf16[256,1024]{1,0:T(8,128)(2,1)S(1)}, bf16[256,1024]{1,0:T(8,128)(2,1)S(1)}, u32[]{:S(2)}, u32[]{:S(2)}) collective-permute-start(bf16[256,1024]{1,0:T(8,128)(2,1)S(1)} %constant_dynamic-slice_fusion.4), channel_id=1, source_target_pairs={{0,1},{1,0},{2,3},{3,2},{4,5},{5,4},{6,7},{7,6},{8,9},{9,8},{10,11... | collective-permute-start | bytes 1572872 | tf_op jit(solution)/shard_map/ppermute | solution.py:205
  352.8 18.9 %slice-start.1 = ((s8[8388608]{0:T(1024)(128)(4,1)}), s8[4194304]{0:T(1024)(128)(4,1)S(1)}, s32[]{:S(2)}) async-start(s8[8388608]{0:T(1024)(128)(4,1)} %bitcast.32), calls=%async_computation.6 | async-start | bytes 8388608
  371.7 3.0 copy-start.8
  374.1 18.0 %collective-permute-start.10 = (bf16[256,1024]{1,0:T(8,128)(2,1)S(1)}, bf16[256,1024]{1,0:T(8,128)(2,1)S(1)}, u32[]{:S(2)}, u32[]{:S(2)}) collective-permute-start(bf16[256,1024]{1,0:T(8,128)(2,1)S(1)} %constant_dynamic-slice_fusion.1), channel_id=1, source_target_pairs={{0,1},{1,0},{2,3},{3,2},{4,5},{5,4},{6,7},{7,6},{8,9},{9,8},{10,11... | collective-permute-start | bytes 1572872 | tf_op jit(solution)/shard_map/ppermute | solution.py:205
  381.6 1.1 copy-start.9
  382.7 15.9 %collective-permute-start.9 = (bf16[256,1024]{1,0:T(8,128)(2,1)}, bf16[256,1024]{1,0:T(8,128)(2,1)S(1)}, u32[]{:S(2)}, u32[]{:S(2)}) collective-permute-start(bf16[256,1024]{1,0:T(8,128)(2,1)} %constant_dynamic-slice_fusion.2), channel_id=1, source_target_pairs={{0,1},{1,0},{2,3},{3,2},{4,5},{5,4},{6,7},{7,6},{8,9},{9,8},{10,11... | collective-permute-start | bytes 1572872 | tf_op jit(solution)/shard_map/ppermute | solution.py:205
  391.8 18.2 %collective-permute-start.11 = (bf16[256,1024]{1,0:T(8,128)(2,1)}, bf16[256,1024]{1,0:T(8,128)(2,1)}, u32[]{:S(2)}, u32[]{:S(2)}) collective-permute-start(bf16[256,1024]{1,0:T(8,128)(2,1)} %constant_dynamic-slice_fusion), channel_id=1, source_target_pairs={{0,1},{1,0},{2,3},{3,2},{4,5},{5,4},{6,7},{7,6},{8,9},{9,8},{10,11... | collective-permute-start | bytes 1572872 | tf_op jit(solution)/shard_map/ppermute | solution.py:205
  411.6 8.7 %copy-start.1 = (bf16[512,2048]{1,0:T(8,128)(2,1)S(1)}, bf16[512,2048]{1,0:T(8,128)(2,1)}, u32[]{:S(2)}) copy-start(bf16[512,2048]{1,0:T(8,128)(2,1)} %param.8) | copy-start | bytes 6291460
Sparse Core Ops, SparseCore 0:
  9.0 46.2 all-gather.9
  56.9 80.4 all-gather.7
  139.0 80.6 all-gather.11
  221.2 45.9 all-gather.13
  268.6 45.8 all-gather.15
